TPU v7x, 512 devices: a whole 4x8x8 slice. The times are simulated.
512 devices in a mesh: prow: 8 (over y), pcol: 64 (over z, x, core).
Axes of the slice: x: 4, y: 8, z: 8, core: 2. Of those that a mesh axis runs over, the one named last changes fastest.
Arguments:
- y_root: float32 [16384, 384], P(('prow', 'pcol')), may hold values from -6 to 6
- root_inverse: float32 [16384, 16384], P('prow', 'pcol'), may hold values from -0.046875 to 0.046875
- coupling: float32 [2, 8192, 8192], P(None, 'pcol', 'prow'), may hold values from -0.0625 to 0.0625
- row_list: int32 [2, 8192], P(None, 'pcol'), may hold values from 0 to 16383, as said below
- y_kids: float32 [2, 8192, 384], P(None, 'prow', 'pcol'), may hold values from -6 to 6
- kid_inverse: float32 [2, 8192, 8192], P(None, 'prow', 'pcol'), may hold values from -0.0625 to 0.0625
Outputs:
- x_root: float32 [16384, 384], P('pcol', 'prow')
- x_kids: float32 [2, 8192, 384], P(None, 'pcol', 'prow')
Inputs may be any that keep to these rules, and one draw needn't show every extreme that they name: `row_list`: split each child's list into blocks of 8192 / 64 consecutive entries; block j names distinct root rows from j * 256 to (j + 1) * 256 - 1, always including the first and the last of them.
All inputs are finite; a program needn't handle non-finite values.
Results may differ from a plain program's by a relative error of at most 0.0001.
Values sent between devices are 32-bit elements; how exact they have to be, the bound alone decides.
No kernel may reach another device: no remote copies, remote signals or barrier semaphores. Data moves between devices by JAX's collectives and lax.ppermute only.
A program may use at most 64 MiB of HBM per device.

v0:
```python
import jax
import jax.numpy as jnp
from jax import lax
from jax.sharding import PartitionSpec as P


def body(y_root, root_inverse, coupling, row_list, y_kids, kid_inverse):
    high = lax.Precision.HIGHEST
    span = root_inverse.shape[1]
    partial_root = lax.dot_general(
        root_inverse,
        lax.all_gather(y_root, "pcol", axis=0, tiled=True),
        (((0,), (0,)), ((), ())),
        precision=high,
        preferred_element_type=jnp.float32,
    )
    x_root = lax.psum_scatter(partial_root, "prow", scatter_dimension=1, tiled=True)
    root_rows = lax.all_gather(x_root, "prow", axis=1, tiled=True)
    local_rows = row_list - lax.axis_index("pcol") * span
    picked = root_rows[local_rows]
    update_part = jnp.einsum(
        "smc,smk->sck", coupling, picked, precision=high, preferred_element_type=jnp.float32
    )
    update = lax.psum_scatter(update_part, "pcol", scatter_dimension=2, tiled=True)
    reduced = lax.all_gather(y_kids - update, "pcol", axis=2, tiled=True)
    kid_part = jnp.einsum(
        "src,srk->sck", kid_inverse, reduced, precision=high, preferred_element_type=jnp.float32
    )
    x_kids = lax.psum_scatter(kid_part, "prow", scatter_dimension=2, tiled=True)
    return (x_root, x_kids)


def solution(mesh):
    in_specs = (
        P(("prow", "pcol"), None),
        P("prow", "pcol"),
        P(None, "pcol", "prow"),
        P(None, "pcol"),
        P(None, "prow", "pcol"),
        P(None, "prow", "pcol"),
    )
    out_specs = (P("pcol", "prow"), P(None, "pcol", "prow"))
    return jax.shard_map(body, mesh=mesh, in_specs=in_specs, out_specs=out_specs, check_vma=False)
```

profile of v0, /device:TPU:1, one launch (start us, length us, event | category | flops | bytes accessed | tf_op | source)
XLA Modules:
  0.0 513.9 jit_solution(1713223856586861939)
XLA Ops:
  7.2 0.0 all-gather.3.cloned.1.call-start
  7.2 0.7 all-gather.3.cloned.1.call-update
  7.9 0.0 reduce-scatter.3.cloned.1.call-start
  8.0 93.9 %all-gather.3.cloned.1.call-done = f32[2048,384]{1,0:T(8,128)} async-done(((f32[32,384]{1,0:T(8,128)}), f32[2048,384]{1,0:T(8,128)}) %all-gather.3.cloned.1.call-update) | async-done | bytes 3145744 | tf_op jit(solution)/shard_map/all_gather | solution.py:12
  101.9 7.7 %fusion.6 = f32[256,384]{0,1:T(8,128)} fusion(f32[2048,256]{1,0:T(8,128)S(1)} %copy-done, f32[2048,384]{1,0:T(8,128)} %all-gather.3.cloned.1.call-done), kind=kOutput, calls=%fused_computation.9 | convolution fusion | flops 2415919104 | bytes 5636096 | tf_op jit(solution)/shard_map/dot_general | solution.py:10
  109.6 0.0 reduce-scatter.3.cloned.1.call-update
  109.6 0.0 all-reduce.3.cloned.1.call-start
  109.7 30.9 %reduce-scatter.3.cloned.1.call-done = f32[256,48]{0,1:T(8,128)} async-done(((f32[256,384]{0,1:T(8,128)}), f32[256,48]{0,1:T(8,128)}) %reduce-scatter.3.cloned.1.call-update) | async-done | bytes 49168 | tf_op jit(solution)/shard_map/reduce_scatter | solution.py:17
  140.6 19.0 %all_gather.10 = f32[256,384]{0,1:T(8,128)S(1)} all-gather(f32[256,48]{0,1:T(8,128)} %reduce-scatter.3.cloned.1.call-done), channel_id=1, replica_groups=mesh['prow'=8,'pcol'=64] {'prow'}, dimensions={1}, use_global_device_ids=true | all-gather | bytes 442368 | tf_op jit(solution)/shard_map/all_gather | solution.py:18
  159.6 0.2 copy.10
  159.7 1.0 gather_fusion
  160.7 3.9 fusion.7
  164.7 4.1 copy.18
  168.8 0.0 all-reduce.3.cloned.1.call-update
  168.8 0.0 all-gather.5.cloned.1.call-start
  168.8 1.3 dynamic-slice
  170.8 210.7 %all-reduce.3.cloned.1.call-done = f32[2,1024,384]{1,0,2:T(2,128)} async-done(((f32[2,1024,384]{1,0,2:T(2,128)}), f32[2,1024,384]{1,0,2:T(2,128)}) %all-reduce.3.cloned.1.call-update) | async-done | bytes 3145744
  381.6 1.4 dynamic-slice_subtract_fusion
  383.0 0.0 all-gather.5.cloned.1.call-update
  383.0 0.2 reduce-scatter.5.cloned.1.call-start
  383.3 86.8 %all-gather.5.cloned.1.call-done = f32[2,1024,384]{1,0,2:T(2,128)} async-done(((f32[2,1024,6]{1,0,2:T(2,128)}), f32[2,1024,384]{1,0,2:T(2,128)}) %all-gather.5.cloned.1.call-update) | async-done | bytes 3145744 | tf_op jit(solution)/shard_map/all_gather | solution.py:25
  470.1 6.3 %fusion.2 = f32[2,128,384]{1,2,0:T(8,128)} fusion(f32[2,1024,128]{2,1,0:T(8,128)S(1)} %copy-done.1, f32[2,1024,384]{1,0,2:T(2,128)} %all-gather.5.cloned.1.call-done), kind=kOutput, calls=%fused_computation.4 | convolution fusion | flops 1207959552 | bytes 4587520 | tf_op jit(solution)/shard_map/src,srk->sck/dot_general | solution.py:26
  476.4 0.0 reduce-scatter.5.cloned.1.call-update
  476.4 31.0 %reduce-scatter.5.cloned.1.call-done = f32[2,128,48]{1,2,0:T(8,128)} async-done(((f32[2,128,384]{1,2,0:T(8,128)}), f32[2,128,48]{1,2,0:T(8,128)}) %reduce-scatter.5.cloned.1.call-update) | async-done | bytes 49168 | tf_op jit(solution)/shard_map/reduce_scatter | solution.py:29
  (10 shorter events, 0.0 us)
Async XLA Ops:
  7.2 94.7 %copy-start = (f32[2048,256]{1,0:T(8,128)S(1)}, f32[2048,256]{1,0:T(8,128)}, u32[]{:S(2)}) copy-start(f32[2048,256]{1,0:T(8,128)} %param.7) | copy-start | bytes 6291460
  7.2 102.5 %copy-start.3 = (s32[2,128]{1,0:T(2,128)S(1)}, s32[2,128]{1,0:T(2,128)}, u32[]{:S(2)}) copy-start(s32[2,128]{1,0:T(2,128)} %param.9) | copy-start | bytes 3076
  7.2 94.7 %all-gather.3.cloned.1.call-start = ((), (), s32[]{:S(2)}) async-start(), calls=%async_computation.2 | async-start | bytes 3194880 | tf_op jit(solution)/shard_map/all_gather | solution.py:12
  7.9 132.7 %reduce-scatter.3.cloned.1.call-start = ((), (), s32[]{:S(2)}) async-start(), calls=%async_computation.3 | async-start | bytes 442368 | tf_op jit(solution)/shard_map/reduce_scatter | solution.py:17
  109.6 272.0 %all-reduce.3.cloned.1.call-start = ((), (), s32[]{:S(2)}) async-start(), calls=%async_computation.6 | async-start | bytes 6291456
  168.8 212.8 %copy-start.2 = (f32[2,1024,6]{1,0,2:T(2,128)S(1)}, f32[2,1024,6]{1,0,2:T(2,128)}, u32[]{:S(2)}) copy-start(f32[2,1024,6]{1,0,2:T(2,128)} %param.10) | copy-start | bytes 147460
  168.8 301.4 %copy-start.1 = (f32[2,1024,128]{2,1,0:T(8,128)S(1)}, f32[2,1024,128]{2,1,0:T(8,128)}, u32[]{:S(2)}) copy-start(f32[2,1024,128]{2,1,0:T(8,128)} %param.11) | copy-start | bytes 3145732
  168.8 301.3 %all-gather.5.cloned.1.call-start = ((), (), s32[]{:S(2)}) async-start(), calls=%async_computation.4 | async-start | bytes 3194880 | tf_op jit(solution)/shard_map/all_gather | solution.py:25
  383.0 124.3 %reduce-scatter.5.cloned.1.call-start = ((), (), s32[]{:S(2)}) async-start(), calls=%async_computation.5 | async-start | bytes 442368 | tf_op jit(solution)/shard_map/reduce_scatter | solution.py:29
Sparse Core Ops, SparseCore 0:
  11.4 90.4 all-gather.2
  109.7 30.8 reduce-scatter.2
  168.9 212.6 all-reduce.2
  385.3 84.7 all-gather.4
  476.5 30.8 reduce-scatter.4
where the time goes:
time: 518 us; the launch traced here: 514 us
  waiting for transfers between devices  454 us (88%)
  blocking collectives  19 us (4%)
  matrix products  17.9 us (3%)
  between operations  14.5 us (3%)
  local copies, waits for them, and re-layouts  6.62 us (1%)
    unnamed x6, waiting for transfers between devices  211 us
    all_gather x1, waiting for transfers between devices, body(): lax.all_gather(y_root, 'pcol', axis=0, tiled=True)  93.9 us
    all_gather x1, waiting for transfers between devices, body(): reduced = lax.all_gather(y_kids - update, 'pcol', axis=2, tiled=True)  86.8 us
    reduce_scatter x1, waiting for transfers between devices, body(): x_kids = lax.psum_scatter(kid_part, 'prow', scatter_dimension=2, tiled=True)  31 us
    reduce_scatter x1, waiting for transfers between devices, body(): lax.psum_scatter(partial_root, 'prow', scatter_dimension=1, tiled=True)  30.9 us
    all_gather x1, blocking collectives, body(): root_rows = lax.all_gather(x_root, 'prow', axis=1, tiled=True)  19 us
  transfers between devices with their start and end apart: 5, of which 5 were waited for; matrix products, arithmetic and copies ran while one was open for 0% of the time, Pallas kernels for 0%

commit v1 on v0

v1 whole, which is shorter than its diff:
```python
import jax
import jax.numpy as jnp
from jax import lax
from jax.sharding import PartitionSpec as P

AXES = ("prow", "pcol")
NY, NZ, NX, NC = 8, 8, 4, 2
HIGH = lax.Precision.HIGHEST


def device(y, z, x, c):
    return ((y * NZ + z) * NX + x) * NC + c


def far_groups():
    return [
        [device(y, 2 * zh + pz, 2 * xh + px, c) for zh in range(NZ // 2) for xh in range(NX // 2)]
        for y in range(NY) for pz in range(2) for px in range(2) for c in range(NC)
    ]


def near_groups():
    groups = []
    for y in range(NY):
        for c in range(NC):
            for a in range(NZ // 2):
                for b in range(NX // 2):
                    zs = sorted(((2 * a + c) % NZ, (2 * a + c + 1) % NZ), key=lambda v: v % 2)
                    xs = sorted(((2 * b + c) % NX, (2 * b + c + 1) % NX), key=lambda v: v % 2)
                    groups.append([device(y, z, x, c) for z in zs for x in xs])
    return groups


def row_groups():
    return [
        [device(y, z, x, c) for y in range(NY)]
        for z in range(NZ) for x in range(NX) for c in range(NC)
    ]


FAR, NEAR, ROW = far_groups(), near_groups(), row_groups()


def exchange(parts, groups):
    return lax.all_to_all(parts, AXES, 0, 0, axis_index_groups=groups)


def gather(part, groups):
    return exchange(jnp.broadcast_to(part[None], (len(groups[0]),) + part.shape), groups)


def scatter_sum(parts, groups):
    return jnp.sum(exchange(parts, groups), axis=0)


def swap(value):
    return lax.ppermute(value, AXES, [(i, i ^ 1) for i in range(NY * NZ * NX * NC)])


def dot(a, b):
    return lax.dot_general(
        a, b, (((0,), (0,)), ((), ())), precision=HIGH, preferred_element_type=jnp.float32
    )


def body(y_root, root_inverse, coupling, row_list, y_kids, kid_inverse):
    rows, samples = y_root.shape
    span = root_inverse.shape[1]
    pcol = lax.axis_index("pcol")
    core = pcol % NC
    own = lax.dynamic_index_in_dim

    held = gather(gather(y_root, FAR), NEAR)
    held = held.reshape(2, 2, NZ // 2, NX // 2, rows, samples).transpose(2, 0, 3, 1, 4, 5)
    held = held.reshape(NZ * NX * rows, samples)
    other = swap(held)
    factor = root_inverse.reshape(NZ * NX, NC, rows, span)
    partial_root = dot(held, own(factor, core, 1, False).reshape(NZ * NX * rows, span))
    partial_root += dot(other, own(factor, 1 - core, 1, False).reshape(NZ * NX * rows, span))
    x_root = scatter_sum(partial_root.reshape(NY, samples // NY, span), ROW)
    root_rows = gather(x_root, ROW).reshape(samples, span).T

    local_rows = row_list - pcol * span
    width = y_kids.shape[2]

    def reduced_part(child):
        picked = root_rows[own(local_rows, child, 0, False)]
        update = dot(own(coupling, child, 0, False), picked)
        placed = lax.dynamic_update_slice(
            jnp.zeros_like(update), own(y_kids, child, 0, False), (0, pcol * width)
        )
        return placed - update

    sent = swap(reduced_part(1 - core))
    part = reduced_part(core) + sent
    part = scatter_sum(part.reshape(4, part.shape[0] // 4, samples), NEAR)
    part = scatter_sum(part.reshape(8, part.shape[0] // 8, samples), FAR)
    reduced = gather(gather(part, FAR), NEAR).reshape(-1, samples)
    other = swap(reduced)
    mine = dot(reduced, own(kid_inverse, core, 0, False))
    theirs = dot(other, own(kid_inverse, 1 - core, 0, False))
    kid_part = jnp.where(core == 0, jnp.stack([mine, theirs]), jnp.stack([theirs, mine]))
    kid_part = kid_part.reshape(2, NY, samples // NY, -1).transpose(1, 0, 2, 3)
    x_kids = scatter_sum(kid_part, ROW)
    return x_root.T, x_kids.transpose(0, 2, 1)


def solution(mesh):
    in_specs = (
        P(("prow", "pcol"), None),
        P("prow", "pcol"),
        P(None, "pcol", "prow"),
        P(None, "pcol"),
        P(None, "prow", "pcol"),
        P(None, "prow", "pcol"),
    )
    out_specs = (P("pcol", "prow"), P(None, "pcol", "prow"))
    return jax.shard_map(body, mesh=mesh, in_specs=in_specs, out_specs=out_specs, check_vma=False)
```

time: 518 us -> 215 us (0.42)
  waiting for transfers between devices: 454 us -> 24.1 us
  blocking collectives: 19 us -> 131 us
  starting transfers between devices: 0.38 us -> 17.9 us
  local copies, waits for them, and re-layouts: 6.62 us -> 23.7 us
  between operations: 14.5 us -> 0.98 us
    unnamed x6 -> x0, waiting for transfers between devices: 211 us -> none
    all_gather x2 -> x0, waiting for transfers between devices: 181 us -> none  [the longest x1 93.9 us: body(): lax.all_gather(y_root, 'pcol', axis=0, tiled=True)]
    all_to_all x0 -> x7, blocking collectives: none -> 131 us  [exchange(): return lax.all_to_all(parts, AXES, 0, 0, axis_index_groups=groups)]
    reduce_scatter x2 -> x0, waiting for transfers between devices: 61.9 us -> none  [the longest x1 31 us: body(): x_kids = lax.psum_scatter(kid_part, 'prow', scatter_dimension=2, tiled=True)]
    all_to_all x0 -> x2, waiting for transfers between devices: none -> 24.1 us  [exchange(): return lax.all_to_all(parts, AXES, 0, 0, axis_index_groups=groups)]
    all_gather x1 -> x0, blocking collectives: 19 us -> none  [body(): root_rows = lax.all_gather(x_root, 'prow', axis=1, tiled=True)]
    all_to_all x0 -> x2, starting transfers between devices: none -> 10.3 us  [exchange(): return lax.all_to_all(parts, AXES, 0, 0, axis_index_groups=groups)]
    dynamic_update_slice x0 -> x2, local copies, waits for them, and re-layouts: none -> 9.85 us  [reduced_part(): lax.dynamic_update_slice(jnp.zeros_like(update), own(y_kids, child, 0, Fa...]
  transfers between devices with their start and end apart: 5 -> 5, of which waited for: 5 -> 2; matrix products, arithmetic and copies ran while one was open for 0% -> 10% of each run, Pallas kernels for 0% -> 0%
where the time goes in v1:
time: 215 us; the launch traced here: 214 us
  blocking collectives  131 us (61%)
  waiting for transfers between devices  24.1 us (11%)
  local copies, waits for them, and re-layouts  23.7 us (11%)
  starting transfers between devices  17.9 us (8%)
  matrix products  16.2 us (8%)
    all_to_all x7, blocking collectives, exchange(): return lax.all_to_all(parts, AXES, 0, 0, axis_index_groups=groups)  131 us
    all_to_all x2, waiting for transfers between devices, exchange(): return lax.all_to_all(parts, AXES, 0, 0, axis_index_groups=groups)  24.1 us
    dot_general x6, matrix products, dot(): lax.dot_general(a, b, (((0,), (0,)), ((), ())), precision=HIGH, preferred...  16.2 us
    all_to_all x2, starting transfers between devices, exchange(): return lax.all_to_all(parts, AXES, 0, 0, axis_index_groups=groups)  10.3 us
    dynamic_update_slice x2, local copies, waits for them, and re-layouts, reduced_part(): lax.dynamic_update_slice(jnp.zeros_like(update), own(y_kids, child, 0, Fa...  9.85 us
    ppermute x3, starting transfers between devices, swap(): lax.ppermute(value, AXES, [(i, i ^ 1) for i in range(NY * NZ * NX * NC)])  7.6 us
  transfers between devices with their start and end apart: 5, of which 2 were waited for; matrix products, arithmetic and copies ran while one was open for 10% of the time, Pallas kernels for 0%

profile of v1, /device:TPU:1, one launch (start us, length us, event | category | flops | bytes accessed | tf_op | source)
XLA Modules:
  0.0 214.4 jit_solution(6271386367717175661)
XLA Ops:
  1.6 24.9 %all_to_all.45 = f32[8,32,384]{2,1,0:T(8,128)S(1)} all-to-all(f32[8,32,384]{2,1,0:T(8,128)S(1)} %broadcast_in_dim.10), channel_id=1, replica_groups={{0,4,16,20,32,36,48,52},{1,5,17,21,33,37,49,53},{2,6,18,22,34,38,50,54}..., dimensions={0} | all-to-all | bytes 786432 | tf_op jit(solution)/shard_map/all_to_all | solution.py:45
  26.7 21.0 %all_to_all.46 = f32[4,8,32,384]{3,2,1,0:T(8,128)S(1)} all-to-all(f32[4,8,32,384]{3,2,1,0:T(8,128)S(1)} %broadcast_in_dim.11), channel_id=1, replica_groups={{0,2,8,10},{4,6,12,14},{16,18,24,26},{20,22,28,30},{32,34,40,42},{36,38..., dimensions={0} | all-to-all | bytes 3145728 | tf_op jit(solution)/shard_map/all_to_all | solution.py:45
  47.8 1.9 collective-permute-start
  49.8 1.7 constant_dynamic-slice_fusion.4
  51.5 1.9 fusion.18
  53.5 3.4 %fusion = f32[384,256]{0,1:T(8,128)S(1)} fusion(f32[256,384]{1,0:T(8,128)S(1)} %fusion.18, f32[1024,256]{1,0:T(8,128)S(1)} %bitcast.79, f32[1024,384]{1,0:T(8,128)} %collective-permute-done), kind=kOutput, calls=%fused_computation.5 | convolution fusion | flops 1208057856 | bytes 3407872 | tf_op jit(solution)/shard_map/dot_general | solution.py:61
  57.8 6.8 %all-to-all-start.2 = ((f32[8,48,256]{2,1,0:T(8,128)}), f32[8,48,256]{2,1,0:T(8,128)S(1)}, u32[]{:S(2)}, u32[]{:S(2)}) async-start(f32[8,48,256]{2,1,0:T(8,128)} %bitcast.7), calls=%async_computation.2 | async-start | bytes 786432 | tf_op jit(solution)/shard_map/all_to_all | solution.py:45
  64.6 15.1 %all-to-all-done.2 = f32[8,48,256]{2,1,0:T(8,128)S(1)} async-done(((f32[8,48,256]{2,1,0:T(8,128)}), f32[8,48,256]{2,1,0:T(8,128)S(1)}, u32[]{:S(2)}, u32[]{:S(2)}) %all-to-all-start.2) | async-done | bytes 393248 | tf_op jit(solution)/shard_map/all_to_all | solution.py:45
  80.5 3.5 %all-to-all-start.3 = ((f32[8,48,256]{2,1,0:T(8,128)}), f32[8,48,256]{2,1,0:T(8,128)S(1)}, u32[]{:S(2)}, u32[]{:S(2)}) async-start(f32[8,48,256]{2,1,0:T(8,128)} %broadcast_in_dim.12), calls=%async_computation.3 | async-start | bytes 786432 | tf_op jit(solution)/shard_map/all_to_all | solution.py:45
  85.0 4.9 %dynamic_update_slice.7 = f32[1024,384]{1,0:T(8,128)S(1)} dynamic-update-slice(f32[1024,384]{1,0:T(8,128)S(1)} %broadcast.44.clone, f32[1024,6]{1,0:T(8,128)S(1)} %bitcast.81, s32[]{:T(128)} %constant.53.clone.1, s32[]{:T(128)S(6)} %select_n.63) | dynamic-update-slice | bytes 49156 | tf_op jit(solution)/shard_map/dynamic_update_slice | solution.py:89
  90.0 9.0 %all-to-all-done.3 = f32[8,48,256]{2,1,0:T(8,128)S(1)} async-done(((f32[8,48,256]{2,1,0:T(8,128)}), f32[8,48,256]{2,1,0:T(8,128)S(1)}, u32[]{:S(2)}, u32[]{:S(2)}) %all-to-all-start.3) | async-done | bytes 393248 | tf_op jit(solution)/shard_map/all_to_all | solution.py:45
  101.7 2.6 %convolution_subtract_fusion = f32[1024,384]{1,0:T(8,128)} fusion(f32[1024,384]{1,0:T(8,128)S(1)} %dynamic_update_slice.7, f32[128,384]{1,0:T(8,128)S(1)} %gather_fusion.1, f32[2,128,1024]{2,1,0:T(8,128)S(1)} %copy-done, s32[]{:T(128)S(6)} %select_n.61), kind=kOutput, calls=%fused_computation.3 | convolution fusion | flops 604372992 | bytes 3866628 | tf_op jit(solution)/shard_map/dot_general | solution.py:61
  104.3 2.4 %collective-permute-start.1 = (f32[1024,384]{1,0:T(8,128)}, f32[1024,384]{1,0:T(8,128)}, u32[]{:S(2)}, u32[]{:S(2)}) collective-permute-start(f32[1024,384]{1,0:T(8,128)} %convolution_subtract_fusion), channel_id=1, source_target_pairs={{0,1},{1,0},{2,3},{3,2},{4,5},{5,4},{6,7},{7,6},{8,9},{9,8},{10,11... | collective-permute-start | bytes 4718600 | tf_op jit(solution)/shard_map/ppermute | solution.py:57
  107.8 4.9 %dynamic_update_slice.6 = f32[1024,384]{1,0:T(8,128)S(1)} dynamic-update-slice(f32[1024,384]{1,0:T(8,128)S(1)} %broadcast.44.clone.1, f32[1024,6]{1,0:T(8,128)S(1)} %bitcast.82, s32[]{:T(128)} %constant.53.clone.1, s32[]{:T(128)S(6)} %select_n.63) | dynamic-update-slice | bytes 49156 | tf_op jit(solution)/shard_map/dynamic_update_slice | solution.py:89
  113.5 2.9 %subtract_add_fusion = f32[1024,384]{1,0:T(8,128)S(1)} fusion(f32[1024,384]{1,0:T(8,128)} %collective-permute-done.1, f32[1024,384]{1,0:T(8,128)S(1)} %dynamic_update_slice.6, f32[128,384]{1,0:T(8,128)S(1)} %gather_fusion, f32[2,128,1024]{2,1,0:T(8,128)S(1)} %copy-done, s32[]{:T(128)S(6)} %select_n.60), kind=kOutput, calls=%fused_computation.2 | convolution fusion | flops 604766208 | bytes 5439492 | tf_op jit(solution)/shard_map/dot_general | solution.py:61
  116.4 16.5 %all_to_all.49 = f32[4,256,384]{2,1,0:T(8,128)S(1)} all-to-all(f32[4,256,384]{2,1,0:T(8,128)S(1)} %bitcast.77), channel_id=1, replica_groups={{0,2,8,10},{4,6,12,14},{16,18,24,26},{20,22,28,30},{32,34,40,42},{36,38..., dimensions={0} | all-to-all | bytes 3145728 | tf_op jit(solution)/shard_map/all_to_all | solution.py:45
  133.0 16.9 %all_to_all.50 = f32[8,32,384]{2,1,0:T(8,128)S(1)} all-to-all(f32[8,32,384]{2,1,0:T(8,128)S(1)} %bitcast.84), channel_id=1, replica_groups={{0,4,16,20,32,36,48,52},{1,5,17,21,33,37,49,53},{2,6,18,22,34,38,50,54}..., dimensions={0} | all-to-all | bytes 786432 | tf_op jit(solution)/shard_map/all_to_all | solution.py:45
  150.0 17.2 %all_to_all.47 = f32[8,32,384]{2,1,0:T(8,128)S(1)} all-to-all(f32[8,32,384]{2,1,0:T(8,128)S(1)} %broadcast_in_dim.13), channel_id=1, replica_groups={{0,4,16,20,32,36,48,52},{1,5,17,21,33,37,49,53},{2,6,18,22,34,38,50,54}..., dimensions={0} | all-to-all | bytes 786432 | tf_op jit(solution)/shard_map/all_to_all | solution.py:45
  167.4 16.5 %all_to_all.48 = f32[4,8,32,384]{3,2,1,0:T(8,128)S(1)} all-to-all(f32[4,8,32,384]{3,2,1,0:T(8,128)S(1)} %broadcast_in_dim.14), channel_id=1, replica_groups={{0,2,8,10},{4,6,12,14},{16,18,24,26},{20,22,28,30},{32,34,40,42},{36,38..., dimensions={0} | all-to-all | bytes 3145728 | tf_op jit(solution)/shard_map/all_to_all | solution.py:45
  183.9 3.3 %collective-permute-start.2 = (f32[1024,384]{1,0:T(8,128)S(1)}, f32[1024,384]{1,0:T(8,128)}, u32[]{:S(2)}, u32[]{:S(2)}) collective-permute-start(f32[1024,384]{1,0:T(8,128)S(1)} %bitcast.72), channel_id=1, source_target_pairs={{0,1},{1,0},{2,3},{3,2},{4,5},{5,4},{6,7},{7,6},{8,9},{9,8},{10,11... | collective-permute-start | bytes 4718600 | tf_op jit(solution)/shard_map/ppermute | solution.py:57
  188.8 2.9 %convolution_bitcast_fusion.1 = f32[1,8,48,128]{3,2,1,0:T(8,128)S(1)} fusion(f32[8,48,1024]{2,1,0:T(8,128)} %bitcast.76, f32[2,1024,128]{2,1,0:T(8,128)} %param.11, s32[]{:T(128)S(6)} %select_n.60), kind=kOutput, calls=%fused_computation.7 | convolution fusion | flops 603979776 | bytes 2293764 | tf_op jit(solution)/shard_map/dot_general | solution.py:61
  191.7 1.9 copy.38
  193.6 2.4 %convolution_bitcast_fusion = f32[1,8,48,128]{3,2,1,0:T(8,128)S(1)} fusion(f32[8,48,1024]{2,1,0:T(8,128)S(1)} %bitcast.74, f32[2,1024,128]{2,1,0:T(8,128)} %param.11, s32[]{:T(128)S(6)} %select_n.61), kind=kOutput, calls=%fused_computation.6 | convolution fusion | flops 603979776 | bytes 2293764 | tf_op jit(solution)/shard_map/dot_general | solution.py:61
  196.1 17.6 %all_to_all.51 = f32[8,2,48,128]{3,2,1,0:T(8,128)S(1)} all-to-all(f32[8,2,48,128]{3,2,1,0:T(8,128)S(1)} %copy.39), channel_id=1, replica_groups={{0,64,128,192,256,320,384,448},{1,65,129,193,257,321,385,449},{2,66,130..., dimensions={0} | all-to-all | bytes 786432 | tf_op jit(solution)/shard_map/all_to_all | solution.py:45
  (39 shorter events, 11.2 us)
Async XLA Ops:
  0.6 101.1 %copy-start = (f32[2,128,1024]{2,1,0:T(8,128)S(1)}, f32[2,128,1024]{2,1,0:T(8,128)}, u32[]{:S(2)}) copy-start(f32[2,128,1024]{2,1,0:T(8,128)} %param.8) | copy-start | bytes 3145732
  47.8 5.6 %collective-permute-start = (f32[1024,384]{1,0:T(8,128)S(1)}, f32[1024,384]{1,0:T(8,128)}, u32[]{:S(2)}, u32[]{:S(2)}) collective-permute-start(f32[1024,384]{1,0:T(8,128)S(1)} %bitcast.70), channel_id=1, source_target_pairs={{0,1},{1,0},{2,3},{3,2},{4,5},{5,4},{6,7},{7,6},{8,9},{9,8},{10,11... | collective-permute-start | bytes 4718600 | tf_op jit(solution)/shard_map/ppermute | solution.py:57
  56.8 27.1 %copy-start.3 = (f32[2,1024,6]{1,0,2:T(2,128)S(1)}, f32[2,1024,6]{1,0,2:T(2,128)}, u32[]{:S(2)}) copy-start(f32[2,1024,6]{1,0,2:T(2,128)} %param.10) | copy-start | bytes 147460
  57.8 21.9 %all-to-all-start.2 = ((f32[8,48,256]{2,1,0:T(8,128)}), f32[8,48,256]{2,1,0:T(8,128)S(1)}, u32[]{:S(2)}, u32[]{:S(2)}) async-start(f32[8,48,256]{2,1,0:T(8,128)} %bitcast.7), calls=%async_computation.2 | async-start | bytes 786432 | tf_op jit(solution)/shard_map/all_to_all | solution.py:45
  79.7 5.2 %copy-start.2 = (f32[48,256]{1,0:T(8,128)}, f32[48,256]{1,0:T(8,128)S(1)}, u32[]{:S(2)}) copy-start(f32[48,256]{1,0:T(8,128)S(1)} %reduce_sum.36) | copy-start | bytes 147460
  80.5 18.5 %all-to-all-start.3 = ((f32[8,48,256]{2,1,0:T(8,128)}), f32[8,48,256]{2,1,0:T(8,128)S(1)}, u32[]{:S(2)}, u32[]{:S(2)}) async-start(f32[8,48,256]{2,1,0:T(8,128)} %broadcast_in_dim.12), calls=%async_computation.3 | async-start | bytes 786432 | tf_op jit(solution)/shard_map/all_to_all | solution.py:45
  84.6 5.3 %copy-start.4 = (s32[2,128]{1,0:T(2,128)S(1)}, s32[2,128]{1,0:T(2,128)}, u32[]{:S(2)}) copy-start(s32[2,128]{1,0:T(2,128)} %param.9) | copy-start | bytes 3076
  99.0 0.8 copy-start.1
  104.3 9.2 %collective-permute-start.1 = (f32[1024,384]{1,0:T(8,128)}, f32[1024,384]{1,0:T(8,128)}, u32[]{:S(2)}, u32[]{:S(2)}) collective-permute-start(f32[1024,384]{1,0:T(8,128)} %convolution_subtract_fusion), channel_id=1, source_target_pairs={{0,1},{1,0},{2,3},{3,2},{4,5},{5,4},{6,7},{7,6},{8,9},{9,8},{10,11... | collective-permute-start | bytes 4718600 | tf_op jit(solution)/shard_map/ppermute | solution.py:57
  183.9 7.9 %collective-permute-start.2 = (f32[1024,384]{1,0:T(8,128)S(1)}, f32[1024,384]{1,0:T(8,128)}, u32[]{:S(2)}, u32[]{:S(2)}) collective-permute-start(f32[1024,384]{1,0:T(8,128)S(1)} %bitcast.72), channel_id=1, source_target_pairs={{0,1},{1,0},{2,3},{3,2},{4,5},{5,4},{6,7},{7,6},{8,9},{9,8},{10,11... | collective-permute-start | bytes 4718600 | tf_op jit(solution)/shard_map/ppermute | solution.py:57

commit v2 on v1

v2 whole, which is shorter than its diff:
```python
import jax
import jax.numpy as jnp
from jax import lax
from jax.sharding import PartitionSpec as P

AXES = ("prow", "pcol")
NY, NZ, NX, NC = 8, 8, 4, 2
PRECISION = lax.Precision.HIGH
pick = lax.dynamic_index_in_dim


def device(y, z, x, c):
    return ((y * NZ + z) * NX + x) * NC + c


def far_groups():
    return [
        [device(y, 2 * zh + pz, 2 * xh + px, c) for zh in range(NZ // 2) for xh in range(NX // 2)]
        for y in range(NY) for pz in range(2) for px in range(2) for c in range(NC)
    ]


def near_groups():
    groups = []
    for y in range(NY):
        for c in range(NC):
            for a in range(NZ // 2):
                for b in range(NX // 2):
                    zs = sorted(((2 * a + c) % NZ, (2 * a + c + 1) % NZ), key=lambda v: v % 2)
                    xs = sorted(((2 * b + c) % NX, (2 * b + c + 1) % NX), key=lambda v: v % 2)
                    groups.append([device(y, z, x, c) for z in zs for x in xs])
    return groups


def row_groups():
    return [
        [device(y, z, x, c) for y in range(NY)]
        for z in range(NZ) for x in range(NX) for c in range(NC)
    ]


def pair_row_groups():
    return [
        [device(y, z, x, c) for y in range(NY) for c in range(NC)]
        for z in range(NZ) for x in range(NX)
    ]


FAR, NEAR, ROW, PAIR_ROW = far_groups(), near_groups(), row_groups(), pair_row_groups()


def exchange(parts, groups):
    return lax.all_to_all(parts, AXES, 0, 0, axis_index_groups=groups)


def gather(part, groups):
    return exchange(jnp.broadcast_to(part[None], (len(groups[0]),) + part.shape), groups)


def scatter_sum(parts, groups):
    return jnp.sum(exchange(parts, groups), axis=0)


def swap(value):
    return lax.ppermute(value, AXES, [(i, i ^ 1) for i in range(NY * NZ * NX * NC)])


def dot(a, b):
    return lax.dot_general(
        a, b, (((0,), (0,)), ((), ())), precision=PRECISION, preferred_element_type=jnp.float32
    )


def body(y_root, root_inverse, coupling, row_list, y_kids, kid_inverse):
    rows, samples = y_root.shape
    span = root_inverse.shape[1]
    width = y_kids.shape[2]
    per = coupling.shape[1]
    prow, pcol = lax.axis_index("prow"), lax.axis_index("pcol")
    core = pcol % NC
    columns = NZ * NX * rows

    factor = root_inverse.reshape(NZ * NX, NC, rows, span)
    near_rows = pick(factor, core, 1, False).reshape(columns, span)
    far_rows = pick(factor, 1 - core, 1, False).reshape(columns, span)
    extended = jnp.concatenate(
        [coupling, y_kids.transpose(0, 2, 1), jnp.zeros((2, 8 - width, coupling.shape[2]))], axis=1
    )
    link, link_other = pick(extended, core, 0, False), swap(pick(extended, 1 - core, 0, False))
    lane = lax.broadcasted_iota(jnp.int32, (8, samples), 1)
    row = lax.broadcasted_iota(jnp.int32, (8, samples), 0)
    spots = [(lane == row + width * q).astype(jnp.float32) for q in (pcol, pcol ^ 1)]
    ahead = dot(jnp.concatenate([link[per:], link_other[per:]]), jnp.concatenate(spots))
    kept, sent = pick(kid_inverse, core, 0, False), swap(pick(kid_inverse, 1 - core, 0, False))
    solve = jnp.concatenate(
        [jnp.where(core == 0, kept, sent), jnp.where(core == 0, sent, kept)], axis=1
    )

    held = gather(y_root, FAR)
    held, near_rows, far_rows = lax.optimization_barrier((held, near_rows, far_rows))
    held = gather(held, NEAR)
    held = held.reshape(2, 2, NZ // 2, NX // 2, rows, samples).transpose(2, 0, 3, 1, 4, 5)
    held = held.reshape(columns, samples)
    partial_root = dot(near_rows, held) + dot(far_rows, swap(held))
    x_part = scatter_sum(partial_root.reshape(NY, span // NY, samples), ROW)
    root_rows = gather(x_part, ROW).reshape(span, samples)
    x_root = lax.dynamic_slice_in_dim(root_rows, prow * (samples // NY), samples // NY, 1)

    local_rows = row_list - pcol * span
    other = swap(root_rows[pick(local_rows, 1 - core, 0, False)])
    total = ahead - dot(link[:per], root_rows[pick(local_rows, core, 0, False)])
    total = total - dot(link_other[:per], other)
    total = scatter_sum(total.reshape(4, columns // 4, samples), NEAR)
    total = scatter_sum(total.reshape(8, rows, samples), FAR)
    reduced = gather(gather(total, FAR), NEAR).reshape(columns, samples)
    solved = lax.optimization_barrier(dot(solve, reduced))
    solved = solved.reshape(NC, -1, NY, samples // NY).transpose(2, 0, 3, 1)
    solved = solved.reshape((NY * NC,) + solved.shape[2:])
    x_kids = exchange(solved, PAIR_ROW).reshape((NY, NC) + solved.shape[1:])
    x_kids = jnp.sum(x_kids, axis=0)
    return x_root, x_kids.transpose(0, 2, 1)


def solution(mesh):
    in_specs = (
        P(("prow", "pcol"), None),
        P("prow", "pcol"),
        P(None, "pcol", "prow"),
        P(None, "pcol"),
        P(None, "prow", "pcol"),
        P(None, "prow", "pcol"),
    )
    out_specs = (P("pcol", "prow"), P(None, "pcol", "prow"))
    return jax.shard_map(body, mesh=mesh, in_specs=in_specs, out_specs=out_specs, check_vma=False)
```

time: 215 us -> 196 us (0.912)
  blocking collectives: 131 us -> 74.3 us
  waiting for transfers between devices: 24.1 us -> 57.9 us
  starting transfers between devices: 17.9 us -> 42.9 us
  local copies, waits for them, and re-layouts: 23.7 us -> 10.2 us
  matrix products: 16.2 us -> 6.12 us
    all_to_all x7 -> x4, blocking collectives: 131 us -> 74.3 us  [exchange(): return lax.all_to_all(parts, AXES, 0, 0, axis_index_groups=groups)]
    all_to_all x2 -> x5, waiting for transfers between devices: 24.1 us -> 53.8 us  [exchange(): return lax.all_to_all(parts, AXES, 0, 0, axis_index_groups=groups)]
    all_to_all x2 -> x5, starting transfers between devices: 10.3 us -> 32.4 us  [exchange(): return lax.all_to_all(parts, AXES, 0, 0, axis_index_groups=groups)]
    dot_general x6, matrix products: 16.2 us -> 6.12 us  [dot(): lax.dot_general(a, b, (((0,), (0,)), ((), ())), precision=PRECISION, pref...]
    dynamic_update_slice x2 -> x0, local copies, waits for them, and re-layouts: 9.85 us -> none  [reduced_part(): lax.dynamic_update_slice(jnp.zeros_like(update), own(y_kids, child, 0, Fa...]
    ppermute x3 -> x4, waiting for transfers between devices: 0.01 us -> 4.06 us  [swap(): lax.ppermute(value, AXES, [(i, i ^ 1) for i in range(NY * NZ * NX * NC)])]
    dot_general x2 -> x0, local copies, waits for them, and re-layouts: 3.5 us -> none  [dot(): lax.dot_general(a, b, (((0,), (0,)), ((), ())), precision=HIGH, preferred...]
    ppermute x3 -> x4, starting transfers between devices: 7.6 us -> 10.5 us  [swap(): lax.ppermute(value, AXES, [(i, i ^ 1) for i in range(NY * NZ * NX * NC)])]
  transfers between devices with their start and end apart: 5 -> 9, of which waited for: 2 -> 8; matrix products, arithmetic and copies ran while one was open for 10% -> 4% of each run, Pallas kernels for 0% -> 0%
where the time goes in v2:
time: 196 us; the launch traced here: 195 us
  blocking collectives  74.3 us (38%)
  waiting for transfers between devices  57.9 us (30%)
  starting transfers between devices  42.9 us (22%)
  local copies, waits for them, and re-layouts  10.2 us (5%)
  matrix products  6.12 us (3%)
  other arithmetic  2.32 us (1%)
    all_to_all x4, blocking collectives, exchange(): return lax.all_to_all(parts, AXES, 0, 0, axis_index_groups=groups)  74.3 us
    all_to_all x5, waiting for transfers between devices, exchange(): return lax.all_to_all(parts, AXES, 0, 0, axis_index_groups=groups)  53.8 us
    all_to_all x5, starting transfers between devices, exchange(): return lax.all_to_all(parts, AXES, 0, 0, axis_index_groups=groups)  32.4 us
    ppermute x4, starting transfers between devices, swap(): lax.ppermute(value, AXES, [(i, i ^ 1) for i in range(NY * NZ * NX * NC)])  10.5 us
    dot_general x6, matrix products, dot(): lax.dot_general(a, b, (((0,), (0,)), ((), ())), precision=PRECISION, pref...  6.12 us
    ppermute x4, waiting for transfers between devices, swap(): lax.ppermute(value, AXES, [(i, i ^ 1) for i in range(NY * NZ * NX * NC)])  4.06 us
  transfers between devices with their start and end apart: 9, of which 8 were waited for; matrix products, arithmetic and copies ran while one was open for 4% of the time, Pallas kernels for 0%

profile of v2, /device:TPU:1, one launch (start us, length us, event | category | flops | bytes accessed | tf_op | source)
XLA Modules:
  0.0 194.7 jit_solution(2939331103436793217)
XLA Ops:
  0.6 1.6 broadcast_in_dim.12
  2.2 13.3 %all-to-all-start = ((f32[8,32,384]{2,1,0:T(8,128)}), f32[8,32,384]{2,1,0:T(8,128)S(1)}, u32[]{:S(2)}, u32[]{:S(2)}) async-start(f32[8,32,384]{2,1,0:T(8,128)} %broadcast_in_dim.12), calls=%async_computation | async-start | bytes 786432 | tf_op jit(solution)/shard_map/all_to_all | solution.py:53
  15.5 1.7 constant_dynamic-slice_fusion.3
  17.2 8.5 %all-to-all-done = f32[8,32,384]{2,1,0:T(8,128)S(1)} async-done(((f32[8,32,384]{2,1,0:T(8,128)}), f32[8,32,384]{2,1,0:T(8,128)S(1)}, u32[]{:S(2)}, u32[]{:S(2)}) %all-to-all-start) | async-done | bytes 393248 | tf_op jit(solution)/shard_map/all_to_all | solution.py:53
  25.9 22.2 %all_to_all.45 = f32[4,8,32,384]{3,2,1,0:T(8,128)S(1)} all-to-all(f32[4,8,32,384]{3,2,1,0:T(8,128)S(1)} %broadcast_in_dim.13), channel_id=1, replica_groups={{0,2,8,10},{4,6,12,14},{16,18,24,26},{20,22,28,30},{32,34,40,42},{36,38..., dimensions={0} | all-to-all | bytes 3145728 | tf_op jit(solution)/shard_map/all_to_all | solution.py:53
  48.2 1.9 collective-permute-start
  51.3 2.2 %collective-permute-done = f32[1024,384]{1,0:T(8,128)S(1)} collective-permute-done((f32[1024,384]{1,0:T(8,128)S(1)}, f32[1024,384]{1,0:T(8,128)S(1)}, u32[]{:S(2)}, u32[]{:S(2)}) %collective-permute-start) | collective-permute-done | bytes 1572896 | tf_op jit(solution)/shard_map/ppermute | solution.py:65
  53.5 1.8 convolution_add_fusion
  55.3 6.8 %all-to-all-start.2 = ((f32[8,32,384]{2,1,0:T(8,128)}), f32[8,32,384]{2,1,0:T(8,128)S(1)}, u32[]{:S(2)}, u32[]{:S(2)}) async-start(f32[8,32,384]{2,1,0:T(8,128)} %bitcast.6), calls=%async_computation.2 | async-start | bytes 786432 | tf_op jit(solution)/shard_map/all_to_all | solution.py:53
  62.4 2.3 %collective-permute-start.2 = (f32[136,1024]{1,0:T(8,128)S(1)}, f32[136,1024]{1,0:T(8,128)S(1)}, u32[]{:S(2)}, u32[]{:S(2)}) collective-permute-start(f32[136,1024]{1,0:T(8,128)S(1)} %dynamic-slice_bitcast_fusion), channel_id=1, source_target_pairs={{0,1},{1,0},{2,3},{3,2},{4,5},{5,4},{6,7},{7,6},{8,9},{9,8},{10,11... | collective-permute-start | bytes 1671176 | tf_op jit(solution)/shard_map/ppermute | solution.py:65
  64.8 12.5 %all-to-all-done.2 = f32[8,32,384]{2,1,0:T(8,128)S(1)} async-done(((f32[8,32,384]{2,1,0:T(8,128)}), f32[8,32,384]{2,1,0:T(8,128)S(1)}, u32[]{:S(2)}, u32[]{:S(2)}) %all-to-all-start.2) | async-done | bytes 393248 | tf_op jit(solution)/shard_map/all_to_all | solution.py:53
  78.1 3.5 %all-to-all-start.3 = ((f32[8,32,384]{2,1,0:T(8,128)}), f32[8,32,384]{2,1,0:T(8,128)S(1)}, u32[]{:S(2)}, u32[]{:S(2)}) async-start(f32[8,32,384]{2,1,0:T(8,128)} %broadcast_in_dim.14), calls=%async_computation.3 | async-start | bytes 786432 | tf_op jit(solution)/shard_map/all_to_all | solution.py:53
  83.1 13.5 %all-to-all-done.3 = f32[8,32,384]{2,1,0:T(8,128)S(1)} async-done(((f32[8,32,384]{2,1,0:T(8,128)}), f32[8,32,384]{2,1,0:T(8,128)S(1)}, u32[]{:S(2)}, u32[]{:S(2)}) %all-to-all-start.3) | async-done | bytes 393248 | tf_op jit(solution)/shard_map/all_to_all | solution.py:53
  98.2 2.5 %collective-permute-start.3 = (f32[128,384]{1,0:T(8,128)S(1)}, f32[128,384]{1,0:T(8,128)S(1)}, u32[]{:S(2)}, u32[]{:S(2)}) collective-permute-start(f32[128,384]{1,0:T(8,128)S(1)} %gather_fusion.1), channel_id=1, source_target_pairs={{0,1},{1,0},{2,3},{3,2},{4,5},{5,4},{6,7},{7,6},{8,9},{9,8},{10,11... | collective-permute-start | bytes 589832 | tf_op jit(solution)/shard_map/ppermute | solution.py:65
  102.6 16.5 %all_to_all.46 = f32[4,256,384]{2,1,0:T(8,128)S(1)} all-to-all(f32[4,256,384]{2,1,0:T(8,128)S(1)} %bitcast.61), channel_id=1, replica_groups={{0,2,8,10},{4,6,12,14},{16,18,24,26},{20,22,28,30},{32,34,40,42},{36,38..., dimensions={0} | all-to-all | bytes 3145728 | tf_op jit(solution)/shard_map/all_to_all | solution.py:53
  119.2 17.5 %all_to_all.47 = f32[8,32,384]{2,1,0:T(8,128)S(1)} all-to-all(f32[8,32,384]{2,1,0:T(8,128)S(1)} %bitcast.67), channel_id=1, replica_groups={{0,4,16,20,32,36,48,52},{1,5,17,21,33,37,49,53},{2,6,18,22,34,38,50,54}..., dimensions={0} | all-to-all | bytes 786432 | tf_op jit(solution)/shard_map/all_to_all | solution.py:53
  136.7 18.2 %all_to_all.48 = f32[8,32,384]{2,1,0:T(8,128)S(1)} all-to-all(f32[8,32,384]{2,1,0:T(8,128)S(1)} %broadcast_in_dim.16), channel_id=1, replica_groups={{0,4,16,20,32,36,48,52},{1,5,17,21,33,37,49,53},{2,6,18,22,34,38,50,54}..., dimensions={0} | all-to-all | bytes 786432 | tf_op jit(solution)/shard_map/all_to_all | solution.py:53
  154.9 1.4 broadcast_in_dim.17
  156.2 3.7 %all-to-all-start.7 = ((f32[4,8,32,384]{3,2,1,0:T(8,128)}), f32[4,8,32,384]{3,2,1,0:T(8,128)S(1)}, u32[]{:S(2)}, u32[]{:S(2)}) async-start(f32[4,8,32,384]{3,2,1,0:T(8,128)} %broadcast_in_dim.17), calls=%async_computation.7 | async-start | bytes 3145728 | tf_op jit(solution)/shard_map/all_to_all | solution.py:53
  160.0 3.7 %collective-permute-start.1 = (f32[1024,128]{1,0:T(8,128)S(1)}, f32[1024,128]{1,0:T(8,128)}, u32[]{:S(2)}, u32[]{:S(2)}) collective-permute-start(f32[1024,128]{1,0:T(8,128)S(1)} %dynamic-slice_bitcast_fusion.3), channel_id=1, source_target_pairs={{0,1},{1,0},{2,3},{3,2},{4,5},{5,4},{6,7},{7,6},{8,9},{9,8},{10,11... | collective-permute-start | bytes 1572872 | tf_op jit(solution)/shard_map/ppermute | solution.py:65
  163.7 1.6 collective-permute-done.1
  166.7 5.6 %all-to-all-done.7 = f32[4,8,32,384]{3,2,1,0:T(8,128)S(1)} async-done(((f32[4,8,32,384]{3,2,1,0:T(8,128)}), f32[4,8,32,384]{3,2,1,0:T(8,128)S(1)}, u32[]{:S(2)}, u32[]{:S(2)}) %all-to-all-start.7) | async-done | bytes 1572896 | tf_op jit(solution)/shard_map/all_to_all | solution.py:53
  174.4 5.1 %all-to-all-start.8 = ((f32[16,48,128]{2,1,0:T(8,128)}), f32[16,48,128]{2,1,0:T(8,128)S(1)}, u32[]{:S(2)}, u32[]{:S(2)}) async-start(f32[16,48,128]{2,1,0:T(8,128)} %bitcast.22), calls=%async_computation.8 | async-start | bytes 786432 | tf_op jit(solution)/shard_map/all_to_all | solution.py:53
  180.3 13.7 %all-to-all-done.8 = f32[16,48,128]{2,1,0:T(8,128)S(1)} async-done(((f32[16,48,128]{2,1,0:T(8,128)}), f32[16,48,128]{2,1,0:T(8,128)S(1)}, u32[]{:S(2)}, u32[]{:S(2)}) %all-to-all-start.8) | async-done | bytes 393248 | tf_op jit(solution)/shard_map/all_to_all | solution.py:53
  (50 shorter events, 12.5 us)
Async XLA Ops:
  2.2 23.5 %all-to-all-start = ((f32[8,32,384]{2,1,0:T(8,128)}), f32[8,32,384]{2,1,0:T(8,128)S(1)}, u32[]{:S(2)}, u32[]{:S(2)}) async-start(f32[8,32,384]{2,1,0:T(8,128)} %broadcast_in_dim.12), calls=%async_computation | async-start | bytes 786432 | tf_op jit(solution)/shard_map/all_to_all | solution.py:53
  48.1 2.1 %copy-start.4 = (f32[2,1024,6]{1,0,2:T(2,128)S(1)}, f32[2,1024,6]{1,0,2:T(2,128)}, u32[]{:S(2)}) copy-start(f32[2,1024,6]{1,0,2:T(2,128)} %param.10) | copy-start | bytes 147460
  48.2 5.3 %collective-permute-start = (f32[1024,384]{1,0:T(8,128)S(1)}, f32[1024,384]{1,0:T(8,128)S(1)}, u32[]{:S(2)}, u32[]{:S(2)}) collective-permute-start(f32[1024,384]{1,0:T(8,128)S(1)} %bitcast.58), channel_id=1, source_target_pairs={{0,1},{1,0},{2,3},{3,2},{4,5},{5,4},{6,7},{7,6},{8,9},{9,8},{10,11... | collective-permute-start | bytes 4718600 | tf_op jit(solution)/shard_map/ppermute | solution.py:65
  51.3 10.8 %copy-start = (f32[2,128,1024]{2,1,0:T(8,128)S(1)}, f32[2,128,1024]{2,1,0:T(8,128)}, u32[]{:S(2)}) copy-start(f32[2,128,1024]{2,1,0:T(8,128)} %param.8) | copy-start | bytes 3145732
  55.3 22.0 %all-to-all-start.2 = ((f32[8,32,384]{2,1,0:T(8,128)}), f32[8,32,384]{2,1,0:T(8,128)S(1)}, u32[]{:S(2)}, u32[]{:S(2)}) async-start(f32[8,32,384]{2,1,0:T(8,128)} %bitcast.6), calls=%async_computation.2 | async-start | bytes 786432 | tf_op jit(solution)/shard_map/all_to_all | solution.py:53
  62.1 2.6 %copy-start.5 = (s32[2,128]{1,0:T(2,128)S(1)}, s32[2,128]{1,0:T(2,128)}, u32[]{:S(2)}) copy-start(s32[2,128]{1,0:T(2,128)} %param.9) | copy-start | bytes 3076
  62.4 19.3 %collective-permute-start.2 = (f32[136,1024]{1,0:T(8,128)S(1)}, f32[136,1024]{1,0:T(8,128)S(1)}, u32[]{:S(2)}, u32[]{:S(2)}) collective-permute-start(f32[136,1024]{1,0:T(8,128)S(1)} %dynamic-slice_bitcast_fusion), channel_id=1, source_target_pairs={{0,1},{1,0},{2,3},{3,2},{4,5},{5,4},{6,7},{7,6},{8,9},{9,8},{10,11... | collective-permute-start | bytes 1671176 | tf_op jit(solution)/shard_map/ppermute | solution.py:65
  78.1 18.5 %all-to-all-start.3 = ((f32[8,32,384]{2,1,0:T(8,128)}), f32[8,32,384]{2,1,0:T(8,128)S(1)}, u32[]{:S(2)}, u32[]{:S(2)}) async-start(f32[8,32,384]{2,1,0:T(8,128)} %broadcast_in_dim.14), calls=%async_computation.3 | async-start | bytes 786432 | tf_op jit(solution)/shard_map/all_to_all | solution.py:53
  81.7 0.8 copy-start.2
  98.2 3.6 %copy-start.3 = (f32[136,1024]{1,0:T(8,128)S(1)}, f32[136,1024]{1,0:T(8,128)}, u32[]{:S(2)}) copy-start(f32[136,1024]{1,0:T(8,128)} %copy-done.2) | copy-start | bytes 1671172
  98.2 3.6 %collective-permute-start.3 = (f32[128,384]{1,0:T(8,128)S(1)}, f32[128,384]{1,0:T(8,128)S(1)}, u32[]{:S(2)}, u32[]{:S(2)}) collective-permute-start(f32[128,384]{1,0:T(8,128)S(1)} %gather_fusion.1), channel_id=1, source_target_pairs={{0,1},{1,0},{2,3},{3,2},{4,5},{5,4},{6,7},{7,6},{8,9},{9,8},{10,11... | collective-permute-start | bytes 589832 | tf_op jit(solution)/shard_map/ppermute | solution.py:65
  156.2 3.7 %copy-start.1 = (f32[2,1024,128]{2,1,0:T(8,128)S(1)}, f32[2,1024,128]{2,1,0:T(8,128)}, u32[]{:S(2)}) copy-start(f32[2,1024,128]{2,1,0:T(8,128)} %param.11) | copy-start | bytes 3145732
  156.2 16.0 %all-to-all-start.7 = ((f32[4,8,32,384]{3,2,1,0:T(8,128)}), f32[4,8,32,384]{3,2,1,0:T(8,128)S(1)}, u32[]{:S(2)}, u32[]{:S(2)}) async-start(f32[4,8,32,384]{3,2,1,0:T(8,128)} %broadcast_in_dim.17), calls=%async_computation.7 | async-start | bytes 3145728 | tf_op jit(solution)/shard_map/all_to_all | solution.py:53
  160.0 5.4 %collective-permute-start.1 = (f32[1024,128]{1,0:T(8,128)S(1)}, f32[1024,128]{1,0:T(8,128)}, u32[]{:S(2)}, u32[]{:S(2)}) collective-permute-start(f32[1024,128]{1,0:T(8,128)S(1)} %dynamic-slice_bitcast_fusion.3), channel_id=1, source_target_pairs={{0,1},{1,0},{2,3},{3,2},{4,5},{5,4},{6,7},{7,6},{8,9},{9,8},{10,11... | collective-permute-start | bytes 1572872 | tf_op jit(solution)/shard_map/ppermute | solution.py:65
  174.4 19.6 %all-to-all-start.8 = ((f32[16,48,128]{2,1,0:T(8,128)}), f32[16,48,128]{2,1,0:T(8,128)S(1)}, u32[]{:S(2)}, u32[]{:S(2)}) async-start(f32[16,48,128]{2,1,0:T(8,128)} %bitcast.22), calls=%async_computation.8 | async-start | bytes 786432 | tf_op jit(solution)/shard_map/all_to_all | solution.py:53

commit v3 on v2

--- a/solution.py
+++ b/solution.py
@@ -87,17 +87,17 @@
         [coupling, y_kids.transpose(0, 2, 1), jnp.zeros((2, 8 - width, coupling.shape[2]))], axis=1
     )
     link, link_other = pick(extended, core, 0, False), swap(pick(extended, 1 - core, 0, False))
+    kept, sent = pick(kid_inverse, core, 0, False), swap(pick(kid_inverse, 1 - core, 0, False))
+
+    held = gather(y_root, FAR)
+    solve = jnp.concatenate(
+        [jnp.where(core == 0, kept, sent), jnp.where(core == 0, sent, kept)], axis=1
+    )
+    held, link_other, solve = lax.optimization_barrier((held, link_other, solve))
     lane = lax.broadcasted_iota(jnp.int32, (8, samples), 1)
     row = lax.broadcasted_iota(jnp.int32, (8, samples), 0)
     spots = [(lane == row + width * q).astype(jnp.float32) for q in (pcol, pcol ^ 1)]
     ahead = dot(jnp.concatenate([link[per:], link_other[per:]]), jnp.concatenate(spots))
-    kept, sent = pick(kid_inverse, core, 0, False), swap(pick(kid_inverse, 1 - core, 0, False))
-    solve = jnp.concatenate(
-        [jnp.where(core == 0, kept, sent), jnp.where(core == 0, sent, kept)], axis=1
-    )
-
-    held = gather(y_root, FAR)
-    held, near_rows, far_rows = lax.optimization_barrier((held, near_rows, far_rows))
     held = gather(held, NEAR)
     held = held.reshape(2, 2, NZ // 2, NX // 2, rows, samples).transpose(2, 0, 3, 1, 4, 5)
     held = held.reshape(columns, samples)

time: 196 us -> 194 us (0.990)
  blocking collectives: 74.3 us -> 91.5 us
  waiting for transfers between devices: 57.9 us -> 47.9 us
  starting transfers between devices: 42.9 us -> 36.4 us
  local copies, waits for them, and re-layouts: 10.2 us -> 6.95 us
    all_to_all x4 -> x5, blocking collectives: 74.3 us -> 91.5 us  [exchange(): return lax.all_to_all(parts, AXES, 0, 0, axis_index_groups=groups)]
    all_to_all x5 -> x4, waiting for transfers between devices: 53.8 us -> 45.7 us  [exchange(): return lax.all_to_all(parts, AXES, 0, 0, axis_index_groups=groups)]
    all_to_all x5 -> x4, starting transfers between devices: 32.4 us -> 27 us  [exchange(): return lax.all_to_all(parts, AXES, 0, 0, axis_index_groups=groups)]
  transfers between devices with their start and end apart: 9 -> 8, of which waited for: 8 -> 6; matrix products, arithmetic and copies ran while one was open for 4% -> 3% of each run, Pallas kernels for 0% -> 0%
where the time goes in v3:
time: 194 us; the launch traced here: 193 us
  blocking collectives  91.5 us (47%)
  waiting for transfers between devices  47.9 us (25%)
  starting transfers between devices  36.4 us (19%)
  local copies, waits for them, and re-layouts  6.95 us (4%)
  matrix products  6.28 us (3%)
  other arithmetic  3.37 us (2%)
    all_to_all x5, blocking collectives, exchange(): return lax.all_to_all(parts, AXES, 0, 0, axis_index_groups=groups)  91.5 us
    all_to_all x4, waiting for transfers between devices, exchange(): return lax.all_to_all(parts, AXES, 0, 0, axis_index_groups=groups)  45.7 us
    all_to_all x4, starting transfers between devices, exchange(): return lax.all_to_all(parts, AXES, 0, 0, axis_index_groups=groups)  27 us
    ppermute x4, starting transfers between devices, swap(): lax.ppermute(value, AXES, [(i, i ^ 1) for i in range(NY * NZ * NX * NC)])  9.37 us
    dot_general x6, matrix products, dot(): lax.dot_general(a, b, (((0,), (0,)), ((), ())), precision=PRECISION, pref...  6.28 us
  transfers between devices with their start and end apart: 8, of which 6 were waited for; matrix products, arithmetic and copies ran while one was open for 3% of the time, Pallas kernels for 0%

profile of v3, /device:TPU:1, one launch (start us, length us, event | category | flops | bytes accessed | tf_op | source)
XLA Modules:
  0.0 193.4 jit_solution(16896658356481553995)
XLA Ops:
  0.7 1.7 broadcast_in_dim.12
  2.4 13.3 %all-to-all-start = ((f32[8,32,384]{2,1,0:T(8,128)}), f32[8,32,384]{2,1,0:T(8,128)S(1)}, u32[]{:S(2)}, u32[]{:S(2)}) async-start(f32[8,32,384]{2,1,0:T(8,128)} %broadcast_in_dim.12), calls=%async_computation | async-start | bytes 786432 | tf_op jit(solution)/shard_map/all_to_all | solution.py:53
  15.8 2.9 %collective-permute-start.1 = (f32[1024,128]{1,0:T(8,128)S(1)}, f32[1024,128]{1,0:T(8,128)}, u32[]{:S(2)}, u32[]{:S(2)}) collective-permute-start(f32[1024,128]{1,0:T(8,128)S(1)} %dynamic-slice_bitcast_fusion.3), channel_id=1, source_target_pairs={{0,1},{1,0},{2,3},{3,2},{4,5},{5,4},{6,7},{7,6},{8,9},{9,8},{10,11... | collective-permute-start | bytes 1572872 | tf_op jit(solution)/shard_map/ppermute | solution.py:65
  19.0 1.9 collective-permute-start
  20.9 1.3 bitcast_select_fusion.1
  22.2 1.0 pad_maximum_fusion
  23.2 2.7 %all-to-all-done = f32[8,32,384]{2,1,0:T(8,128)S(1)} async-done(((f32[8,32,384]{2,1,0:T(8,128)}), f32[8,32,384]{2,1,0:T(8,128)S(1)}, u32[]{:S(2)}, u32[]{:S(2)}) %all-to-all-start) | async-done | bytes 393248 | tf_op jit(solution)/shard_map/all_to_all | solution.py:53
  26.1 22.2 %all_to_all.45 = f32[4,8,32,384]{3,2,1,0:T(8,128)S(1)} all-to-all(f32[4,8,32,384]{3,2,1,0:T(8,128)S(1)} %broadcast_in_dim.14), channel_id=1, replica_groups={{0,2,8,10},{4,6,12,14},{16,18,24,26},{20,22,28,30},{32,34,40,42},{36,38..., dimensions={0} | all-to-all | bytes 3145728 | tf_op jit(solution)/shard_map/all_to_all | solution.py:53
  48.4 2.1 %collective-permute-start.2 = (f32[1024,384]{1,0:T(8,128)S(1)}, f32[1024,384]{1,0:T(8,128)S(1)}, u32[]{:S(2)}, u32[]{:S(2)}) collective-permute-start(f32[1024,384]{1,0:T(8,128)S(1)} %bitcast.58), channel_id=1, source_target_pairs={{0,1},{1,0},{2,3},{3,2},{4,5},{5,4},{6,7},{7,6},{8,9},{9,8},{10,11... | collective-permute-start | bytes 4718600 | tf_op jit(solution)/shard_map/ppermute | solution.py:65
  50.7 1.1 fusion.16
  51.9 2.0 %collective-permute-done.2 = f32[1024,384]{1,0:T(8,128)S(1)} collective-permute-done((f32[1024,384]{1,0:T(8,128)S(1)}, f32[1024,384]{1,0:T(8,128)S(1)}, u32[]{:S(2)}, u32[]{:S(2)}) %collective-permute-start.2) | collective-permute-done | bytes 1572896 | tf_op jit(solution)/shard_map/ppermute | solution.py:65
  53.9 1.9 convolution_add_fusion
  55.7 6.8 %all-to-all-start.2 = ((f32[8,32,384]{2,1,0:T(8,128)}), f32[8,32,384]{2,1,0:T(8,128)S(1)}, u32[]{:S(2)}, u32[]{:S(2)}) async-start(f32[8,32,384]{2,1,0:T(8,128)} %bitcast.10), calls=%async_computation.2 | async-start | bytes 786432 | tf_op jit(solution)/shard_map/all_to_all | solution.py:53
  62.6 15.1 %all-to-all-done.2 = f32[8,32,384]{2,1,0:T(8,128)S(1)} async-done(((f32[8,32,384]{2,1,0:T(8,128)}), f32[8,32,384]{2,1,0:T(8,128)S(1)}, u32[]{:S(2)}, u32[]{:S(2)}) %all-to-all-start.2) | async-done | bytes 393248 | tf_op jit(solution)/shard_map/all_to_all | solution.py:53
  78.5 3.5 %all-to-all-start.3 = ((f32[8,32,384]{2,1,0:T(8,128)}), f32[8,32,384]{2,1,0:T(8,128)S(1)}, u32[]{:S(2)}, u32[]{:S(2)}) async-start(f32[8,32,384]{2,1,0:T(8,128)} %broadcast_in_dim.15), calls=%async_computation.3 | async-start | bytes 786432 | tf_op jit(solution)/shard_map/all_to_all | solution.py:53
  82.7 14.3 %all-to-all-done.3 = f32[8,32,384]{2,1,0:T(8,128)S(1)} async-done(((f32[8,32,384]{2,1,0:T(8,128)}), f32[8,32,384]{2,1,0:T(8,128)S(1)}, u32[]{:S(2)}, u32[]{:S(2)}) %all-to-all-start.3) | async-done | bytes 393248 | tf_op jit(solution)/shard_map/all_to_all | solution.py:53
  98.6 2.5 %collective-permute-start.3 = (f32[128,384]{1,0:T(8,128)S(1)}, f32[128,384]{1,0:T(8,128)S(1)}, u32[]{:S(2)}, u32[]{:S(2)}) collective-permute-start(f32[128,384]{1,0:T(8,128)S(1)} %gather_fusion.1), channel_id=1, source_target_pairs={{0,1},{1,0},{2,3},{3,2},{4,5},{5,4},{6,7},{7,6},{8,9},{9,8},{10,11... | collective-permute-start | bytes 589832 | tf_op jit(solution)/shard_map/ppermute | solution.py:65
  103.0 16.5 %all_to_all.46 = f32[4,256,384]{2,1,0:T(8,128)S(1)} all-to-all(f32[4,256,384]{2,1,0:T(8,128)S(1)} %bitcast.62), channel_id=1, replica_groups={{0,2,8,10},{4,6,12,14},{16,18,24,26},{20,22,28,30},{32,34,40,42},{36,38..., dimensions={0} | all-to-all | bytes 3145728 | tf_op jit(solution)/shard_map/all_to_all | solution.py:53
  119.6 17.5 %all_to_all.47 = f32[8,32,384]{2,1,0:T(8,128)S(1)} all-to-all(f32[8,32,384]{2,1,0:T(8,128)S(1)} %bitcast.68), channel_id=1, replica_groups={{0,4,16,20,32,36,48,52},{1,5,17,21,33,37,49,53},{2,6,18,22,34,38,50,54}..., dimensions={0} | all-to-all | bytes 786432 | tf_op jit(solution)/shard_map/all_to_all | solution.py:53
  137.1 18.1 %all_to_all.48 = f32[8,32,384]{2,1,0:T(8,128)S(1)} all-to-all(f32[8,32,384]{2,1,0:T(8,128)S(1)} %broadcast_in_dim.16), channel_id=1, replica_groups={{0,4,16,20,32,36,48,52},{1,5,17,21,33,37,49,53},{2,6,18,22,34,38,50,54}..., dimensions={0} | all-to-all | bytes 786432 | tf_op jit(solution)/shard_map/all_to_all | solution.py:53
  155.4 17.3 %all_to_all.49 = f32[4,8,32,384]{3,2,1,0:T(8,128)S(1)} all-to-all(f32[4,8,32,384]{3,2,1,0:T(8,128)S(1)} %broadcast_in_dim.17), channel_id=1, replica_groups={{0,2,8,10},{4,6,12,14},{16,18,24,26},{20,22,28,30},{32,34,40,42},{36,38..., dimensions={0} | all-to-all | bytes 3145728 | tf_op jit(solution)/shard_map/all_to_all | solution.py:53
  172.7 1.0 fusion.17
  174.9 3.4 %all-to-all-start.8 = ((f32[16,48,128]{2,1,0:T(8,128)}), f32[16,48,128]{2,1,0:T(8,128)S(1)}, u32[]{:S(2)}, u32[]{:S(2)}) async-start(f32[16,48,128]{2,1,0:T(8,128)} %bitcast.22), calls=%async_computation.8 | async-start | bytes 786432 | tf_op jit(solution)/shard_map/all_to_all | solution.py:53
  179.1 13.6 %all-to-all-done.8 = f32[16,48,128]{2,1,0:T(8,128)S(1)} async-done(((f32[16,48,128]{2,1,0:T(8,128)}), f32[16,48,128]{2,1,0:T(8,128)S(1)}, u32[]{:S(2)}, u32[]{:S(2)}) %all-to-all-start.8) | async-done | bytes 393248 | tf_op jit(solution)/shard_map/all_to_all | solution.py:53
  (54 shorter events, 8.8 us)
Async XLA Ops:
  0.6 15.1 %copy-start.3 = (f32[2,1024,128]{2,1,0:T(8,128)S(1)}, f32[2,1024,128]{2,1,0:T(8,128)}, u32[]{:S(2)}) copy-start(f32[2,1024,128]{2,1,0:T(8,128)} %param.11) | copy-start | bytes 3145732
  0.6 18.0 %copy-start.6 = (f32[2,1024,6]{1,0,2:T(2,128)S(1)}, f32[2,1024,6]{1,0,2:T(2,128)}, u32[]{:S(2)}) copy-start(f32[2,1024,6]{1,0,2:T(2,128)} %param.10) | copy-start | bytes 147460
  0.7 18.1 %copy-start.2 = (f32[2,128,1024]{2,1,0:T(8,128)S(1)}, f32[2,128,1024]{2,1,0:T(8,128)}, u32[]{:S(2)}) copy-start(f32[2,128,1024]{2,1,0:T(8,128)} %param.8) | copy-start | bytes 3145732
  2.4 23.5 %all-to-all-start = ((f32[8,32,384]{2,1,0:T(8,128)}), f32[8,32,384]{2,1,0:T(8,128)S(1)}, u32[]{:S(2)}, u32[]{:S(2)}) async-start(f32[8,32,384]{2,1,0:T(8,128)} %broadcast_in_dim.12), calls=%async_computation | async-start | bytes 786432 | tf_op jit(solution)/shard_map/all_to_all | solution.py:53
  15.8 5.1 %collective-permute-start.1 = (f32[1024,128]{1,0:T(8,128)S(1)}, f32[1024,128]{1,0:T(8,128)}, u32[]{:S(2)}, u32[]{:S(2)}) collective-permute-start(f32[1024,128]{1,0:T(8,128)S(1)} %dynamic-slice_bitcast_fusion.3), channel_id=1, source_target_pairs={{0,1},{1,0},{2,3},{3,2},{4,5},{5,4},{6,7},{7,6},{8,9},{9,8},{10,11... | collective-permute-start | bytes 1572872 | tf_op jit(solution)/shard_map/ppermute | solution.py:65
  19.0 4.3 %collective-permute-start = (f32[136,1024]{1,0:T(8,128)S(1)}, f32[136,1024]{1,0:T(8,128)S(1)}, u32[]{:S(2)}, u32[]{:S(2)}) collective-permute-start(f32[136,1024]{1,0:T(8,128)S(1)} %dynamic-slice_bitcast_fusion), channel_id=1, source_target_pairs={{0,1},{1,0},{2,3},{3,2},{4,5},{5,4},{6,7},{7,6},{8,9},{9,8},{10,11... | collective-permute-start | bytes 1671176 | tf_op jit(solution)/shard_map/ppermute | solution.py:65
  23.2 58.9 %copy-start.4 = (f32[136,1024]{1,0:T(8,128)}, f32[136,1024]{1,0:T(8,128)S(1)}, u32[]{:S(2)}) copy-start(f32[136,1024]{1,0:T(8,128)S(1)} %collective-permute-done) | copy-start | bytes 1671172
  48.3 2.2 %copy-start.1 = (f32[2048,256]{1,0:T(8,128)S(1)}, f32[2048,256]{1,0:T(8,128)}, u32[]{:S(2)}) copy-start(f32[2048,256]{1,0:T(8,128)} %param.7) | copy-start | bytes 6291460
  48.4 5.4 %collective-permute-start.2 = (f32[1024,384]{1,0:T(8,128)S(1)}, f32[1024,384]{1,0:T(8,128)S(1)}, u32[]{:S(2)}, u32[]{:S(2)}) collective-permute-start(f32[1024,384]{1,0:T(8,128)S(1)} %bitcast.58), channel_id=1, source_target_pairs={{0,1},{1,0},{2,3},{3,2},{4,5},{5,4},{6,7},{7,6},{8,9},{9,8},{10,11... | collective-permute-start | bytes 4718600 | tf_op jit(solution)/shard_map/ppermute | solution.py:65
  53.9 8.7 %copy-start.7 = (s32[2,128]{1,0:T(2,128)S(1)}, s32[2,128]{1,0:T(2,128)}, u32[]{:S(2)}) copy-start(s32[2,128]{1,0:T(2,128)} %param.9) | copy-start | bytes 3076
  55.7 22.0 %all-to-all-start.2 = ((f32[8,32,384]{2,1,0:T(8,128)}), f32[8,32,384]{2,1,0:T(8,128)S(1)}, u32[]{:S(2)}, u32[]{:S(2)}) async-start(f32[8,32,384]{2,1,0:T(8,128)} %bitcast.10), calls=%async_computation.2 | async-start | bytes 786432 | tf_op jit(solution)/shard_map/all_to_all | solution.py:53
  78.5 18.5 %all-to-all-start.3 = ((f32[8,32,384]{2,1,0:T(8,128)}), f32[8,32,384]{2,1,0:T(8,128)S(1)}, u32[]{:S(2)}, u32[]{:S(2)}) async-start(f32[8,32,384]{2,1,0:T(8,128)} %broadcast_in_dim.15), calls=%async_computation.3 | async-start | bytes 786432 | tf_op jit(solution)/shard_map/all_to_all | solution.py:53
  98.5 3.6 %copy-start.5 = (f32[136,1024]{1,0:T(8,128)S(1)}, f32[136,1024]{1,0:T(8,128)}, u32[]{:S(2)}) copy-start(f32[136,1024]{1,0:T(8,128)} %copy-done.4) | copy-start | bytes 1671172
  98.6 3.6 %collective-permute-start.3 = (f32[128,384]{1,0:T(8,128)S(1)}, f32[128,384]{1,0:T(8,128)S(1)}, u32[]{:S(2)}, u32[]{:S(2)}) collective-permute-start(f32[128,384]{1,0:T(8,128)S(1)} %gather_fusion.1), channel_id=1, source_target_pairs={{0,1},{1,0},{2,3},{3,2},{4,5},{5,4},{6,7},{7,6},{8,9},{9,8},{10,11... | collective-permute-start | bytes 589832 | tf_op jit(solution)/shard_map/ppermute | solution.py:65
  155.4 17.3 %copy-start = (f32[1024,256]{1,0:T(8,128)S(1)}, f32[1024,256]{1,0:T(8,128)}, u32[]{:S(2)}) copy-start(f32[1024,256]{1,0:T(8,128)} %pad_maximum_fusion) | copy-start | bytes 3145732
  174.9 17.9 %all-to-all-start.8 = ((f32[16,48,128]{2,1,0:T(8,128)}), f32[16,48,128]{2,1,0:T(8,128)S(1)}, u32[]{:S(2)}, u32[]{:S(2)}) async-start(f32[16,48,128]{2,1,0:T(8,128)} %bitcast.22), calls=%async_computation.8 | async-start | bytes 786432 | tf_op jit(solution)/shard_map/all_to_all | solution.py:53

commit v4 on v3

--- a/solution.py
+++ b/solution.py
@@ -65,6 +65,14 @@
     return lax.ppermute(value, AXES, [(i, i ^ 1) for i in range(NY * NZ * NX * NC)])
 
 
+def halve(value, bit):
+    side = lax.axis_index("prow") // bit % 2
+    sent = lax.ppermute(
+        pick(value, 1 - side, 1, False), "prow", [(i, i ^ bit) for i in range(NY)]
+    )
+    return pick(value, side, 1, False) + sent
+
+
 def dot(a, b):
     return lax.dot_general(
         a, b, (((0,), (0,)), ((), ())), precision=PRECISION, preferred_element_type=jnp.float32
@@ -76,7 +84,7 @@
     span = root_inverse.shape[1]
     width = y_kids.shape[2]
     per = coupling.shape[1]
-    prow, pcol = lax.axis_index("prow"), lax.axis_index("pcol")
+    pcol = lax.axis_index("pcol")
     core = pcol % NC
     columns = NZ * NX * rows
 
@@ -87,13 +95,13 @@
         [coupling, y_kids.transpose(0, 2, 1), jnp.zeros((2, 8 - width, coupling.shape[2]))], axis=1
     )
     link, link_other = pick(extended, core, 0, False), swap(pick(extended, 1 - core, 0, False))
-    kept, sent = pick(kid_inverse, core, 0, False), swap(pick(kid_inverse, 1 - core, 0, False))
 
     held = gather(y_root, FAR)
-    solve = jnp.concatenate(
-        [jnp.where(core == 0, kept, sent), jnp.where(core == 0, sent, kept)], axis=1
-    )
-    held, link_other, solve = lax.optimization_barrier((held, link_other, solve))
+    held, link_other = lax.optimization_barrier((held, link_other))
+    own, other = (v[:per].reshape(NY, 1, per // NY, -1) for v in (link, link_other))
+    links = jnp.where(
+        core == 0, jnp.concatenate([own, other], axis=1), jnp.concatenate([other, own], axis=1)
+    ).reshape(2 * per, -1)
     lane = lax.broadcasted_iota(jnp.int32, (8, samples), 1)
     row = lax.broadcasted_iota(jnp.int32, (8, samples), 0)
     spots = [(lane == row + width * q).astype(jnp.float32) for q in (pcol, pcol ^ 1)]
@@ -102,23 +110,34 @@
     held = held.reshape(2, 2, NZ // 2, NX // 2, rows, samples).transpose(2, 0, 3, 1, 4, 5)
     held = held.reshape(columns, samples)
     partial_root = dot(near_rows, held) + dot(far_rows, swap(held))
-    x_part = scatter_sum(partial_root.reshape(NY, span // NY, samples), ROW)
-    root_rows = gather(x_part, ROW).reshape(span, samples)
-    x_root = lax.dynamic_slice_in_dim(root_rows, prow * (samples // NY), samples // NY, 1)
-
-    local_rows = row_list - pcol * span
-    other = swap(root_rows[pick(local_rows, 1 - core, 0, False)])
-    total = ahead - dot(link[:per], root_rows[pick(local_rows, core, 0, False)])
-    total = total - dot(link_other[:per], other)
+    share = per // NY
+    spots = (row_list - pcol * span).reshape(2, NY, share).transpose(1, 0, 2)
+    picked = partial_root[spots.reshape(-1)].reshape(NY, 2 * share, samples)
+    picked, kid_inverse = lax.optimization_barrier((picked, kid_inverse))
+    kept, sent = pick(kid_inverse, core, 0, False), swap(pick(kid_inverse, 1 - core, 0, False))
+    solve = jnp.concatenate(
+        [jnp.where(core == 0, kept, sent), jnp.where(core == 0, sent, kept)], axis=1
+    )
+    picked, x_root = lax.optimization_barrier((scatter_sum(picked, ROW), partial_root.T))
+    picked = jnp.broadcast_to(picked.reshape(1, 2, share, samples), (NY, 2, share, samples))
+    picked = exchange(picked.reshape(2 * NY, share, samples), PAIR_ROW).reshape(-1, samples)
+    picked, solve = lax.optimization_barrier((picked, solve))
+    total = ahead - dot(links, picked)
     total = scatter_sum(total.reshape(4, columns // 4, samples), NEAR)
-    total = scatter_sum(total.reshape(8, rows, samples), FAR)
-    reduced = gather(gather(total, FAR), NEAR).reshape(columns, samples)
+    total = exchange(total.reshape(8, rows, samples), FAR)
+    x_root = halve(x_root.reshape(4, 2, samples // NY, span), 1)
+    total, x_root = lax.optimization_barrier((total, x_root))
+    total = gather(jnp.sum(total, axis=0), FAR)
+    x_root = halve(x_root.reshape(2, 2, samples // NY, span), 2)
+    total, x_root = lax.optimization_barrier((total, x_root))
+    reduced = gather(total, NEAR).reshape(columns, samples)
+    reduced, x_root = lax.optimization_barrier((reduced, halve(x_root[None], 4)[0]))
     solved = lax.optimization_barrier(dot(solve, reduced))
     solved = solved.reshape(NC, -1, NY, samples // NY).transpose(2, 0, 3, 1)
     solved = solved.reshape((NY * NC,) + solved.shape[2:])
     x_kids = exchange(solved, PAIR_ROW).reshape((NY, NC) + solved.shape[1:])
     x_kids = jnp.sum(x_kids, axis=0)
-    return x_root, x_kids.transpose(0, 2, 1)
+    return x_root.T, x_kids.transpose(0, 2, 1)
 
 
 def solution(mesh):

time: 194 us -> 193 us (level)
  blocking collectives: 91.5 us -> 57.1 us
  starting transfers between devices: 36.4 us -> 51.3 us
  waiting for transfers between devices: 47.9 us -> 57.4 us
  local copies, waits for them, and re-layouts: 6.95 us -> 12.8 us
    all_to_all x5 -> x3, blocking collectives: 91.5 us -> 57.1 us  [exchange(): return lax.all_to_all(parts, AXES, 0, 0, axis_index_groups=groups)]
    ppermute x0 -> x3, waiting for transfers between devices: none -> 17.3 us  [halve(): lax.ppermute(pick(value, 1 - side, 1, False), 'prow', [(i, i ^ bit) for i...]
    all_to_all x4 -> x6, starting transfers between devices: 27 us -> 36.1 us  [exchange(): return lax.all_to_all(parts, AXES, 0, 0, axis_index_groups=groups)]
    ppermute x0 -> x3, starting transfers between devices: none -> 8.07 us  [halve(): lax.ppermute(pick(value, 1 - side, 1, False), 'prow', [(i, i ^ bit) for i...]
    all_to_all x4 -> x6, waiting for transfers between devices: 45.7 us -> 38 us  [exchange(): return lax.all_to_all(parts, AXES, 0, 0, axis_index_groups=groups)]
    ppermute x4 -> x3, starting transfers between devices: 9.37 us -> 7.12 us  [swap(): lax.ppermute(value, AXES, [(i, i ^ 1) for i in range(NY * NZ * NX * NC)])]
    dot_general x6 -> x5, matrix products: 6.28 us -> 7.48 us  [dot(): lax.dot_general(a, b, (((0,), (0,)), ((), ())), precision=PRECISION, pref...]
    broadcast_in_dim x5 -> x4, local copies, waits for them, and re-layouts: 2.88 us -> 3.95 us  [gather(): jnp.broadcast_to(part[None], (len(groups[0]),) + part.shape)]
  transfers between devices with their start and end apart: 8 -> 12, of which waited for: 6 -> 11; matrix products, arithmetic and copies ran while one was open for 3% -> 6% of each run, Pallas kernels for 0% -> 0%
where the time goes in v4:
time: 193 us; the launch traced here: 192 us
  waiting for transfers between devices  57.4 us (30%)
  blocking collectives  57.1 us (30%)
  starting transfers between devices  51.3 us (27%)
  local copies, waits for them, and re-layouts  12.8 us (7%)
  matrix products  7.48 us (4%)
  other arithmetic  4.7 us (2%)
    all_to_all x3, blocking collectives, exchange(): return lax.all_to_all(parts, AXES, 0, 0, axis_index_groups=groups)  57.1 us
    all_to_all x6, waiting for transfers between devices, exchange(): return lax.all_to_all(parts, AXES, 0, 0, axis_index_groups=groups)  38 us
    all_to_all x6, starting transfers between devices, exchange(): return lax.all_to_all(parts, AXES, 0, 0, axis_index_groups=groups)  36.1 us
    ppermute x3, waiting for transfers between devices, halve(): lax.ppermute(pick(value, 1 - side, 1, False), 'prow', [(i, i ^ bit) for i...  17.3 us
    ppermute x3, starting transfers between devices, halve(): lax.ppermute(pick(value, 1 - side, 1, False), 'prow', [(i, i ^ bit) for i...  8.07 us
    dot_general x5, matrix products, dot(): lax.dot_general(a, b, (((0,), (0,)), ((), ())), precision=PRECISION, pref...  7.48 us
    ppermute x3, starting transfers between devices, swap(): lax.ppermute(value, AXES, [(i, i ^ 1) for i in range(NY * NZ * NX * NC)])  7.12 us
    broadcast_in_dim x4, local copies, waits for them, and re-layouts, gather(): jnp.broadcast_to(part[None], (len(groups[0]),) + part.shape)  3.95 us
  transfers between devices with their start and end apart: 12, of which 11 were waited for; matrix products, arithmetic and copies ran while one was open for 6% of the time, Pallas kernels for 0%

profile of v4, /device:TPU:1, one launch (start us, length us, event | category | flops | bytes accessed | tf_op | source)
XLA Modules:
  0.0 191.8 jit_solution(13770711652368999713)
XLA Ops:
  2.3 13.3 %all-to-all-start = ((f32[8,32,384]{2,1,0:T(8,128)}), f32[8,32,384]{2,1,0:T(8,128)S(1)}, u32[]{:S(2)}, u32[]{:S(2)}) async-start(f32[8,32,384]{2,1,0:T(8,128)} %broadcast_in_dim.15), calls=%async_computation | async-start | bytes 786432 | tf_op jit(solution)/shard_map/all_to_all | solution.py:53
  16.7 2.9 %collective-permute-start = (f32[136,1024]{1,0:T(8,128)S(1)}, f32[136,1024]{1,0:T(8,128)}, u32[]{:S(2)}, u32[]{:S(2)}) collective-permute-start(f32[136,1024]{1,0:T(8,128)S(1)} %dynamic-slice_bitcast_fusion), channel_id=1, source_target_pairs={{0,1},{1,0},{2,3},{3,2},{4,5},{5,4},{6,7},{7,6},{8,9},{9,8},{10,11... | collective-permute-start | bytes 1671176 | tf_op jit(solution)/shard_map/ppermute | solution.py:65
  21.3 4.5 %all-to-all-done = f32[8,32,384]{2,1,0:T(8,128)S(1)} async-done(((f32[8,32,384]{2,1,0:T(8,128)}), f32[8,32,384]{2,1,0:T(8,128)S(1)}, u32[]{:S(2)}, u32[]{:S(2)}) %all-to-all-start) | async-done | bytes 393248 | tf_op jit(solution)/shard_map/all_to_all | solution.py:53
  26.0 22.2 %all_to_all.45 = f32[4,8,32,384]{3,2,1,0:T(8,128)S(1)} all-to-all(f32[4,8,32,384]{3,2,1,0:T(8,128)S(1)} %broadcast_in_dim.16), channel_id=1, replica_groups={{0,2,8,10},{4,6,12,14},{16,18,24,26},{20,22,28,30},{32,34,40,42},{36,38..., dimensions={0} | all-to-all | bytes 3145728 | tf_op jit(solution)/shard_map/all_to_all | solution.py:53
  53.8 2.5 %convolution_add_fusion = f32[256,384]{1,0:T(8,128)S(1)} fusion(f32[256,384]{1,0:T(8,128)S(1)} %fusion.9, f32[1024,256]{1,0:T(8,128)S(1)} %bitcast.66, f32[1024,384]{1,0:T(8,128)} %collective-permute-done.1), kind=kOutput, calls=%fused_computation.2 | convolution fusion | flops 604078080 | bytes 3407872 | tf_op jit(solution)/shard_map/dot_general | solution.py:77
  58.0 6.8 %all-to-all-start.2 = ((f32[8,32,384]{2,1,0:T(8,128)}), f32[8,32,384]{2,1,0:T(8,128)S(1)}, u32[]{:S(2)}, u32[]{:S(2)}) async-start(f32[8,32,384]{2,1,0:T(8,128)} %bitcast.14), calls=%async_computation.2 | async-start | bytes 786432 | tf_op jit(solution)/shard_map/all_to_all | solution.py:53
  65.8 2.3 %collective-permute-start.2 = (f32[1024,128]{1,0:T(8,128)}, f32[1024,128]{1,0:T(8,128)}, u32[]{:S(2)}, u32[]{:S(2)}) collective-permute-start(f32[1024,128]{1,0:T(8,128)} %dynamic-slice_bitcast_fusion.1), channel_id=1, source_target_pairs={{0,1},{1,0},{2,3},{3,2},{4,5},{5,4},{6,7},{7,6},{8,9},{9,8},{10,11... | collective-permute-start | bytes 1572872 | tf_op jit(solution)/shard_map/ppermute | solution.py:65
  68.2 11.8 %all-to-all-done.2 = f32[8,32,384]{2,1,0:T(8,128)S(1)} async-done(((f32[8,32,384]{2,1,0:T(8,128)}), f32[8,32,384]{2,1,0:T(8,128)S(1)}, u32[]{:S(2)}, u32[]{:S(2)}) %all-to-all-start.2) | async-done | bytes 393248 | tf_op jit(solution)/shard_map/all_to_all | solution.py:53
  80.8 3.8 %all-to-all-start.3 = ((f32[16,16,384]{2,1,0:T(8,128)}), f32[16,16,384]{2,1,0:T(8,128)S(1)}, u32[]{:S(2)}, u32[]{:S(2)}) async-start(f32[16,16,384]{2,1,0:T(8,128)} %bitcast.17), calls=%async_computation.3 | async-start | bytes 786432 | tf_op jit(solution)/shard_map/all_to_all | solution.py:53
  89.4 9.8 %all-to-all-done.3 = f32[16,16,384]{2,1,0:T(8,128)S(1)} async-done(((f32[16,16,384]{2,1,0:T(8,128)}), f32[16,16,384]{2,1,0:T(8,128)S(1)}, u32[]{:S(2)}, u32[]{:S(2)}) %all-to-all-start.3) | async-done | bytes 393248 | tf_op jit(solution)/shard_map/all_to_all | solution.py:53
  99.2 2.3 %convolution_subtract_fusion = f32[1024,384]{1,0:T(8,128)S(1)} fusion(f32[1024,384]{1,0:T(8,128)S(1)} %fusion, f32[256,1024]{1,0:T(8,128)} %bitcast.67, f32[256,384]{1,0:T(8,128)S(1)} %bitcast.71), kind=kOutput, calls=%fused_computation.1 | convolution fusion | flops 604372992 | bytes 4587520 | tf_op jit(solution)/shard_map/dot_general | solution.py:77
  101.4 16.5 %all_to_all.46 = f32[4,256,384]{2,1,0:T(8,128)S(1)} all-to-all(f32[4,256,384]{2,1,0:T(8,128)S(1)} %bitcast.63), channel_id=1, replica_groups={{0,2,8,10},{4,6,12,14},{16,18,24,26},{20,22,28,30},{32,34,40,42},{36,38..., dimensions={0} | all-to-all | bytes 3145728 | tf_op jit(solution)/shard_map/all_to_all | solution.py:53
  118.7 3.5 %all-to-all-start.5 = ((f32[8,32,384]{2,1,0:T(8,128)}), f32[8,32,384]{2,1,0:T(8,128)S(1)}, u32[]{:S(2)}, u32[]{:S(2)}) async-start(f32[8,32,384]{2,1,0:T(8,128)} %bitcast.22), calls=%async_computation.5 | async-start | bytes 786432 | tf_op jit(solution)/shard_map/all_to_all | solution.py:53
  124.4 5.3 %collective-permute-done.3 = f32[4,48,256]{2,1,0:T(8,128)S(1)} collective-permute-done((f32[4,48,256]{2,1,0:T(8,128)S(1)}, f32[4,48,256]{2,1,0:T(8,128)S(1)}, u32[]{:S(2)}, u32[]{:S(2)}) %collective-permute-start.3) | collective-permute-done | bytes 196640 | tf_op jit(solution)/shard_map/ppermute | solution.py:70
  129.7 4.8 %all-to-all-done.5 = f32[8,32,384]{2,1,0:T(8,128)S(1)} async-done(((f32[8,32,384]{2,1,0:T(8,128)}), f32[8,32,384]{2,1,0:T(8,128)S(1)}, u32[]{:S(2)}, u32[]{:S(2)}) %all-to-all-start.5) | async-done | bytes 393248 | tf_op jit(solution)/shard_map/all_to_all | solution.py:53
  135.2 5.1 %all-to-all-start.6 = ((f32[8,32,384]{2,1,0:T(8,128)}), f32[8,32,384]{2,1,0:T(8,128)S(1)}, u32[]{:S(2)}, u32[]{:S(2)}) async-start(f32[8,32,384]{2,1,0:T(8,128)} %broadcast_in_dim.19), calls=%async_computation.6 | async-start | bytes 786432 | tf_op jit(solution)/shard_map/all_to_all | solution.py:53
  140.4 3.2 %collective-permute-start.4 = (f32[2,48,256]{2,1,0:T(8,128)S(1)}, f32[2,48,256]{2,1,0:T(8,128)S(1)}, u32[]{:S(2)}, u32[]{:S(2)}) collective-permute-start(f32[2,48,256]{2,1,0:T(8,128)S(1)} %dynamic-slice_bitcast_fusion.3), channel_id=1, source_target_pairs={{0,128},{64,192},{128,0},{192,64},{256,384},{320,448},{384,256},{4... | collective-permute-start | bytes 294920 | tf_op jit(solution)/shard_map/ppermute | solution.py:70
  143.6 6.2 %collective-permute-done.4 = f32[2,48,256]{2,1,0:T(8,128)S(1)} collective-permute-done((f32[2,48,256]{2,1,0:T(8,128)S(1)}, f32[2,48,256]{2,1,0:T(8,128)S(1)}, u32[]{:S(2)}, u32[]{:S(2)}) %collective-permute-start.4) | collective-permute-done | bytes 98336 | tf_op jit(solution)/shard_map/ppermute | solution.py:70
  149.7 4.4 %all-to-all-done.6 = f32[8,32,384]{2,1,0:T(8,128)S(1)} async-done(((f32[8,32,384]{2,1,0:T(8,128)}), f32[8,32,384]{2,1,0:T(8,128)S(1)}, u32[]{:S(2)}, u32[]{:S(2)}) %all-to-all-start.6) | async-done | bytes 393248 | tf_op jit(solution)/shard_map/all_to_all | solution.py:53
  155.4 3.6 %all-to-all-start.7 = ((f32[4,8,32,384]{3,2,1,0:T(8,128)}), f32[4,8,32,384]{3,2,1,0:T(8,128)S(1)}, u32[]{:S(2)}, u32[]{:S(2)}) async-start(f32[4,8,32,384]{3,2,1,0:T(8,128)} %broadcast_in_dim.20), calls=%async_computation.7 | async-start | bytes 3145728 | tf_op jit(solution)/shard_map/all_to_all | solution.py:53
  159.1 2.9 %collective-permute-start.5 = (f32[1,48,256]{2,1,0:T(8,128)S(1)}, f32[1,48,256]{2,1,0:T(8,128)S(1)}, u32[]{:S(2)}, u32[]{:S(2)}) collective-permute-start(f32[1,48,256]{2,1,0:T(8,128)S(1)} %constant_dynamic-slice_fusion), channel_id=1, source_target_pairs={{0,256},{64,320},{128,384},{192,448},{256,0},{320,64},{384,128},{4... | collective-permute-start | bytes 147464 | tf_op jit(solution)/shard_map/ppermute | solution.py:70
  162.0 5.8 %collective-permute-done.5 = f32[1,48,256]{2,1,0:T(8,128)S(1)} collective-permute-done((f32[1,48,256]{2,1,0:T(8,128)S(1)}, f32[1,48,256]{2,1,0:T(8,128)S(1)}, u32[]{:S(2)}, u32[]{:S(2)}) %collective-permute-start.5) | collective-permute-done | bytes 49184 | tf_op jit(solution)/shard_map/ppermute | solution.py:70
  168.5 2.8 %all-to-all-done.7 = f32[4,8,32,384]{3,2,1,0:T(8,128)S(1)} async-done(((f32[4,8,32,384]{3,2,1,0:T(8,128)}), f32[4,8,32,384]{3,2,1,0:T(8,128)S(1)}, u32[]{:S(2)}, u32[]{:S(2)}) %all-to-all-start.7) | async-done | bytes 1572896 | tf_op jit(solution)/shard_map/all_to_all | solution.py:53
  172.7 18.4 %all_to_all.47 = f32[16,48,128]{2,1,0:T(8,128)S(1)} all-to-all(f32[16,48,128]{2,1,0:T(8,128)S(1)} %bitcast.76), channel_id=1, replica_groups={{0,1,64,65,128,129,192,193,256,257,320,321,384,385,448,449},{2,3,66,67,..., dimensions={0} | all-to-all | bytes 786432 | tf_op jit(solution)/shard_map/all_to_all | solution.py:53
  (60 shorter events, 26.2 us)
Async XLA Ops:
  0.6 15.9 %copy-start = (f32[2,128,1024]{2,1,0:T(8,128)S(1)}, f32[2,128,1024]{2,1,0:T(8,128)}, u32[]{:S(2)}) copy-start(f32[2,128,1024]{2,1,0:T(8,128)} %param.8) | copy-start | bytes 3145732
  2.3 23.5 %all-to-all-start = ((f32[8,32,384]{2,1,0:T(8,128)}), f32[8,32,384]{2,1,0:T(8,128)S(1)}, u32[]{:S(2)}, u32[]{:S(2)}) async-start(f32[8,32,384]{2,1,0:T(8,128)} %broadcast_in_dim.15), calls=%async_computation | async-start | bytes 786432 | tf_op jit(solution)/shard_map/all_to_all | solution.py:53
  16.7 4.6 %collective-permute-start = (f32[136,1024]{1,0:T(8,128)S(1)}, f32[136,1024]{1,0:T(8,128)}, u32[]{:S(2)}, u32[]{:S(2)}) collective-permute-start(f32[136,1024]{1,0:T(8,128)S(1)} %dynamic-slice_bitcast_fusion), channel_id=1, source_target_pairs={{0,1},{1,0},{2,3},{3,2},{4,5},{5,4},{6,7},{7,6},{8,9},{9,8},{10,11... | collective-permute-start | bytes 1671176 | tf_op jit(solution)/shard_map/ppermute | solution.py:65
  48.2 2.1 %copy-start.3 = (s32[2,128]{1,0:T(2,128)S(1)}, s32[2,128]{1,0:T(2,128)}, u32[]{:S(2)}) copy-start(s32[2,128]{1,0:T(2,128)} %param.9) | copy-start | bytes 3076
  48.3 5.4 %collective-permute-start.1 = (f32[1024,384]{1,0:T(8,128)S(1)}, f32[1024,384]{1,0:T(8,128)}, u32[]{:S(2)}, u32[]{:S(2)}) collective-permute-start(f32[1024,384]{1,0:T(8,128)S(1)} %bitcast.61), channel_id=1, source_target_pairs={{0,1},{1,0},{2,3},{3,2},{4,5},{5,4},{6,7},{7,6},{8,9},{9,8},{10,11... | collective-permute-start | bytes 4718600 | tf_op jit(solution)/shard_map/ppermute | solution.py:65
  56.3 8.7 %copy-start.1 = (f32[2,1024,128]{2,1,0:T(8,128)S(1)}, f32[2,1024,128]{2,1,0:T(8,128)}, u32[]{:S(2)}) copy-start(f32[2,1024,128]{2,1,0:T(8,128)} %param.11) | copy-start | bytes 3145732
  58.0 22.0 %all-to-all-start.2 = ((f32[8,32,384]{2,1,0:T(8,128)}), f32[8,32,384]{2,1,0:T(8,128)S(1)}, u32[]{:S(2)}, u32[]{:S(2)}) async-start(f32[8,32,384]{2,1,0:T(8,128)} %bitcast.14), calls=%async_computation.2 | async-start | bytes 786432 | tf_op jit(solution)/shard_map/all_to_all | solution.py:53
  65.8 22.4 %collective-permute-start.2 = (f32[1024,128]{1,0:T(8,128)}, f32[1024,128]{1,0:T(8,128)}, u32[]{:S(2)}, u32[]{:S(2)}) collective-permute-start(f32[1024,128]{1,0:T(8,128)} %dynamic-slice_bitcast_fusion.1), channel_id=1, source_target_pairs={{0,1},{1,0},{2,3},{3,2},{4,5},{5,4},{6,7},{7,6},{8,9},{9,8},{10,11... | collective-permute-start | bytes 1572872 | tf_op jit(solution)/shard_map/ppermute | solution.py:65
  80.8 18.4 %all-to-all-start.3 = ((f32[16,16,384]{2,1,0:T(8,128)}), f32[16,16,384]{2,1,0:T(8,128)S(1)}, u32[]{:S(2)}, u32[]{:S(2)}) async-start(f32[16,16,384]{2,1,0:T(8,128)} %bitcast.17), calls=%async_computation.3 | async-start | bytes 786432 | tf_op jit(solution)/shard_map/all_to_all | solution.py:53
  86.5 1.7 copy-start.2
  118.7 15.7 %all-to-all-start.5 = ((f32[8,32,384]{2,1,0:T(8,128)}), f32[8,32,384]{2,1,0:T(8,128)S(1)}, u32[]{:S(2)}, u32[]{:S(2)}) async-start(f32[8,32,384]{2,1,0:T(8,128)} %bitcast.22), calls=%async_computation.5 | async-start | bytes 786432 | tf_op jit(solution)/shard_map/all_to_all | solution.py:53
  122.4 7.2 %collective-permute-start.3 = (f32[4,48,256]{2,1,0:T(8,128)S(1)}, f32[4,48,256]{2,1,0:T(8,128)S(1)}, u32[]{:S(2)}, u32[]{:S(2)}) collective-permute-start(f32[4,48,256]{2,1,0:T(8,128)S(1)} %dynamic-slice_bitcast_fusion.2), channel_id=1, source_target_pairs={{0,64},{64,0},{128,192},{192,128},{256,320},{320,256},{384,448},{4... | collective-permute-start | bytes 589832 | tf_op jit(solution)/shard_map/ppermute | solution.py:70
  135.2 18.9 %all-to-all-start.6 = ((f32[8,32,384]{2,1,0:T(8,128)}), f32[8,32,384]{2,1,0:T(8,128)S(1)}, u32[]{:S(2)}, u32[]{:S(2)}) async-start(f32[8,32,384]{2,1,0:T(8,128)} %broadcast_in_dim.19), calls=%async_computation.6 | async-start | bytes 786432 | tf_op jit(solution)/shard_map/all_to_all | solution.py:53
  140.4 9.4 %collective-permute-start.4 = (f32[2,48,256]{2,1,0:T(8,128)S(1)}, f32[2,48,256]{2,1,0:T(8,128)S(1)}, u32[]{:S(2)}, u32[]{:S(2)}) collective-permute-start(f32[2,48,256]{2,1,0:T(8,128)S(1)} %dynamic-slice_bitcast_fusion.3), channel_id=1, source_target_pairs={{0,128},{64,192},{128,0},{192,64},{256,384},{320,448},{384,256},{4... | collective-permute-start | bytes 294920 | tf_op jit(solution)/shard_map/ppermute | solution.py:70
  155.4 15.8 %all-to-all-start.7 = ((f32[4,8,32,384]{3,2,1,0:T(8,128)}), f32[4,8,32,384]{3,2,1,0:T(8,128)S(1)}, u32[]{:S(2)}, u32[]{:S(2)}) async-start(f32[4,8,32,384]{3,2,1,0:T(8,128)} %broadcast_in_dim.20), calls=%async_computation.7 | async-start | bytes 3145728 | tf_op jit(solution)/shard_map/all_to_all | solution.py:53
  159.1 8.8 %collective-permute-start.5 = (f32[1,48,256]{2,1,0:T(8,128)S(1)}, f32[1,48,256]{2,1,0:T(8,128)S(1)}, u32[]{:S(2)}, u32[]{:S(2)}) collective-permute-start(f32[1,48,256]{2,1,0:T(8,128)S(1)} %constant_dynamic-slice_fusion), channel_id=1, source_target_pairs={{0,256},{64,320},{128,384},{192,448},{256,0},{320,64},{384,128},{4... | collective-permute-start | bytes 147464 | tf_op jit(solution)/shard_map/ppermute | solution.py:70
